TPU v7x, 256 devices: a whole 4x4x8 slice. The times are simulated.
256 devices in a mesh: ctx: 64 (over x, y, z_hi, core), tp: 4 (over z_lo).
Axes of the slice: x: 4, y: 4, z: 8 (z_hi: 2, z_lo: 4; z = z_hi * 4 + z_lo), core: 2. Of those that a mesh axis runs over, the one named last changes fastest.
Arguments:
- query_rows: bfloat16 [8192, 2048], P('ctx', 'tp'), may hold values from -16 to 16
- key_rows: bfloat16 [8192, 2048], P('ctx', 'tp'), may hold values from -6 to 6
- value_rows: bfloat16 [8192, 2048], P('ctx', 'tp'), may hold values from -6 to 6
- long_filter: float32 [8192, 2048], P('ctx', 'tp'), may hold values from -24 to 24
- out_weight: bfloat16 [2048, 4096], P(None, 'tp'), may hold values from -0.125 to 0.125
- grad_out: bfloat16 [8192, 4096], P('ctx', 'tp'), may hold values from -1.5 to 1.5
Outputs:
- output: bfloat16 [8192, 4096], P('ctx', 'tp')
- grad_query: bfloat16 [8192, 2048], P('ctx', 'tp')
- grad_key: bfloat16 [8192, 2048], P('ctx', 'tp')
- grad_value: bfloat16 [8192, 2048], P('ctx', 'tp')
- grad_filter: float32 [8192, 2048], P('ctx', 'tp')
- grad_weight: float32 [2048, 4096], P('ctx', 'tp')
All inputs are finite; a program needn't handle non-finite values.
Results may differ from a plain program's by a relative error of at most 0.0049.
Values may be sent and summed in bfloat16 or wider, within the bound.
A program may use at most 128 MiB of HBM per device.

v0:
```python
import math

import jax
import jax.numpy as jnp
from jax import lax
from jax.sharding import PartitionSpec as P

highest = lax.Precision.HIGHEST


def rotate(values, cosine_part, sine_part):
    real_part = values[..., 0, :, :]
    imag_part = values[..., 1, :, :]
    return jnp.stack(
        [
            real_part * cosine_part - imag_part * sine_part,
            real_part * sine_part + imag_part * cosine_part,
        ],
        axis=-3,
    )


def bit_reverse(number, bit_count):
    flipped = number * 0
    for bit_index in range(bit_count):
        flipped = flipped + ((number >> bit_index & 1) << bit_count - 1 - bit_index)
    return flipped


def position_angle(row_count, device, length):
    position = device * row_count + jnp.arange(row_count, dtype=jnp.int32)
    phase_angle = math.pi / length * position.astype(jnp.float32)
    return (jnp.cos(phase_angle)[:, None], jnp.sin(phase_angle)[:, None])


def modulate(signal, device, length):
    cosine_part, sine_part = position_angle(signal.shape[0], device, length)
    even_part = jnp.stack([signal, jnp.zeros_like(signal)])
    odd_part = jnp.stack([signal * cosine_part, -signal * sine_part])
    return jnp.stack([even_part, odd_part])


def demodulate(spectra, device, length):
    cosine_part, sine_part = position_angle(spectra.shape[-2], device, length)
    summed = spectra[:, 0, 0] + cosine_part * spectra[:, 1, 0] - sine_part * spectra[:, 1, 1]
    return summed / (2.0 * length)


def local_dft(values, direction):
    row_count = values.shape[-2]
    row_index = jnp.arange(row_count, dtype=jnp.int32)
    phase_table = row_index[:, None] * row_index[None, :] % row_count
    phase_angle = 2.0 * math.pi / row_count * phase_table.astype(jnp.float32)
    cosine_table = jnp.cos(phase_angle)
    sine_table = jnp.sin(phase_angle)
    real_part = values[:, :, 0]
    imag_part = values[:, :, 1]

    def apply_table(matrix, part):
        return jnp.einsum("km,srmc->srkc", matrix, part, precision=highest)

    new_real = apply_table(cosine_table, real_part) - direction * apply_table(sine_table, imag_part)
    new_imag = apply_table(cosine_table, imag_part) + direction * apply_table(sine_table, real_part)
    return jnp.stack([new_real, new_imag], axis=2)


def cross_table(ctx_count, bit_count):
    column = jnp.arange(ctx_count, dtype=jnp.int32)
    return column[None, :] * bit_reverse(column, bit_count)[:, None] % ctx_count


def cross_mix(spread, phase_table, direction):
    ctx_count = phase_table.shape[0]
    phase_angle = 2.0 * math.pi / ctx_count * phase_table.astype(jnp.float32)
    cosine_table = jnp.cos(phase_angle)
    sine_table = jnp.sin(phase_angle)
    real_part = spread[:, :, 0]
    imag_part = spread[:, :, 1]

    def apply_table(matrix, part):
        return jnp.einsum("jp,srpbc->srjbc", matrix, part, precision=highest)

    new_real = apply_table(cosine_table, real_part) - direction * apply_table(sine_table, imag_part)
    new_imag = apply_table(cosine_table, imag_part) + direction * apply_table(sine_table, real_part)
    return jnp.stack([new_real, new_imag], axis=2)


def twiddle(values, flipped, length, direction):
    row_count = values.shape[-2]
    row_index = jnp.arange(row_count, dtype=jnp.int32)
    phase_table = row_index * flipped % length
    phase_angle = direction * 2.0 * math.pi / length * phase_table.astype(jnp.float32)
    return rotate(values, jnp.cos(phase_angle)[:, None], jnp.sin(phase_angle)[:, None])


def forward_transform(values):
    ctx_count = lax.axis_size("ctx")
    bit_count = ctx_count.bit_length() - 1
    device = lax.axis_index("ctx")
    length = values.shape[-2] * ctx_count
    phase_table = cross_table(ctx_count, bit_count)
    combined = cross_mix(
        lax.all_to_all(values[:, :, :, None], "ctx", split_axis=4, concat_axis=3, tiled=True),
        phase_table,
        -1.0,
    )
    result = lax.all_to_all(combined, "ctx", split_axis=3, concat_axis=4, tiled=True)
    values = result[:, :, :, 0]
    values = twiddle(values, bit_reverse(device, bit_count), length, -1.0)
    return local_dft(values, -1.0)


def inverse_transform(values):
    ctx_count = lax.axis_size("ctx")
    bit_count = ctx_count.bit_length() - 1
    device = lax.axis_index("ctx")
    length = values.shape[-2] * ctx_count
    values = local_dft(values, 1.0)
    values = twiddle(values, bit_reverse(device, bit_count), length, 1.0)
    phase_table = cross_table(ctx_count, bit_count).T
    combined = cross_mix(
        lax.all_to_all(values[:, :, :, None], "ctx", split_axis=4, concat_axis=3, tiled=True),
        phase_table,
        1.0,
    )
    result = lax.all_to_all(combined, "ctx", split_axis=3, concat_axis=4, tiled=True)
    return result[:, :, :, 0]


def complex_product(left_spec, right_spec, conjugate):
    left_real = left_spec[:, 0]
    left_imag = left_spec[:, 1]
    if conjugate:
        left_imag = -left_imag
    right_real = right_spec[:, 0]
    right_imag = right_spec[:, 1]
    new_real = left_real * right_real - left_imag * right_imag
    new_imag = left_real * right_imag + left_imag * right_real
    return jnp.stack([new_real, new_imag], axis=1)


def per_device(query_rows, key_rows, value_rows, long_filter, out_weight, grad_out):
    ctx_count = lax.axis_size("ctx")
    device = lax.axis_index("ctx")
    row_count = query_rows.shape[0]
    length = row_count * ctx_count
    query_float = query_rows.astype(jnp.float32)
    key_float = key_rows.astype(jnp.float32)
    value_float = value_rows.astype(jnp.float32)
    gated_input = key_float * value_float
    stacked = jnp.stack(
        [modulate(gated_input, device, length), modulate(long_filter, device, length)]
    )
    spectra = forward_transform(stacked)
    gated_spec = spectra[0]
    filter_spec = spectra[1]
    product = complex_product(filter_spec, gated_spec, False)
    convolved = demodulate(inverse_transform(product[None]), device, length)[0]
    mixed_rows = (query_float * convolved).astype(jnp.bfloat16)
    every_channel = lax.all_gather(mixed_rows, "tp", axis=1, tiled=True)
    output = jnp.dot(every_channel, out_weight, preferred_element_type=jnp.float32).astype(
        jnp.bfloat16
    )
    partial_value = lax.dot_general(
        grad_out, out_weight, (((1,), (1,)), ((), ())), preferred_element_type=jnp.float32
    )
    grad_mixed = lax.psum_scatter(partial_value, "tp", scatter_dimension=1, tiled=True)
    grad_query = (grad_mixed * convolved).astype(jnp.bfloat16)
    grad_conv = grad_mixed * query_float
    grad_spec = forward_transform(modulate(grad_conv, device, length)[None])[0]
    back_gated = complex_product(filter_spec, grad_spec, True)
    back_filter = complex_product(gated_spec, grad_spec, True)
    adjoint = demodulate(inverse_transform(jnp.stack([back_gated, back_filter])), device, length)
    grad_gated = adjoint[0]
    grad_filter = adjoint[1]
    grad_key = (grad_gated * value_float).astype(jnp.bfloat16)
    grad_value = (grad_gated * key_float).astype(jnp.bfloat16)
    grad_weight = lax.psum_scatter(
        lax.dot_general(
            every_channel, grad_out, (((0,), (0,)), ((), ())), preferred_element_type=jnp.float32
        ),
        "ctx",
        scatter_dimension=0,
        tiled=True,
    )
    return (output, grad_query, grad_key, grad_value, grad_filter, grad_weight)


def solution(mesh):
    return jax.shard_map(
        per_device,
        mesh=mesh,
        in_specs=(
            P("ctx", "tp"),
            P("ctx", "tp"),
            P("ctx", "tp"),
            P("ctx", "tp"),
            P(None, "tp"),
            P("ctx", "tp"),
        ),
        out_specs=(
            P("ctx", "tp"),
            P("ctx", "tp"),
            P("ctx", "tp"),
            P("ctx", "tp"),
            P("ctx", "tp"),
            P("ctx", "tp"),
        ),
        check_vma=False,
    )
```

profile of v0, /device:TPU:96, one launch (start us, length us, event | category | flops | bytes accessed | tf_op | source)
XLA Modules:
  0.0 844.5 jit_solution(5752257944953129623)
XLA Ops:
  8.1 4.7 fusion.330
  12.9 31.8 %reduce-scatter.3.cloned.1.call-done = f32[128,512]{1,0:T(8,128)} async-done(((f32[128,2048]{1,0:T(8,128)}), f32[128,512]{1,0:T(8,128)}) %reduce-scatter.3.cloned.1.call-update) | async-done | bytes 262160 | tf_op jit(solution)/shard_map/reduce_scatter | solution.py:167
  47.8 12.7 %all-to-all-start.4 = ((f32[1,2,2,1,128,512]{5,2,1,3,0,4:T(2,128)}), f32[1,2,2,1,128,512]{5,2,1,3,0,4:T(2,128)S(1)}, u32[]{:S(2)}, u32[]{:S(2)}) async-start(f32[1,2,2,1,128,512]{5,2,1,3,0,4:T(2,128)} %copy.105), calls=%async_computation.5 | async-start | bytes 2097152 | tf_op jit(solution)/shard_map/all_to_all | solution.py:103
  61.3 3.0 copy.84
  64.2 27.7 %all-to-all-done.4 = f32[1,2,2,1,128,512]{5,2,1,3,0,4:T(2,128)S(1)} async-done(((f32[1,2,2,1,128,512]{5,2,1,3,0,4:T(2,128)}), f32[1,2,2,1,128,512]{5,2,1,3,0,4:T(2,128)S(1)}, u32[]{:S(2)}, u32[]{:S(2)}) %all-to-all-start.4) | async-done | bytes 1048608 | tf_op jit(solution)/shard_map/all_to_all | solution.py:103
  91.9 4.7 all-to-all-start
  103.2 27.9 %all-to-all-done = f32[2,2,2,1,128,512]{5,2,1,0,3,4:T(2,128)S(1)} async-done(((f32[2,2,2,1,128,512]{5,2,1,0,3,4:T(2,128)}), f32[2,2,2,1,128,512]{5,2,1,0,3,4:T(2,128)S(1)}, u32[]{:S(2)}, u32[]{:S(2)}) %all-to-all-start) | async-done | bytes 2097184 | tf_op jit(solution)/shard_map/all_to_all | solution.py:103
  131.1 20.7 %all-to-all-start.5 = ((f32[1,2,2,64,2,512]{5,4,1,2,0,3:T(2,128)}), f32[1,2,2,64,2,512]{5,4,1,2,0,3:T(2,128)S(1)}, u32[]{:S(2)}, u32[]{:S(2)}) async-start(f32[1,2,2,64,2,512]{5,4,1,2,0,3:T(2,128)} %copy.109), calls=%async_computation.6 | async-start | bytes 2097152 | tf_op jit(solution)/shard_map/all_to_all | solution.py:107
  162.1 3.0 copy.88
  165.1 9.2 %all-to-all-done.5 = f32[1,2,2,64,2,512]{5,4,1,2,0,3:T(2,128)S(1)} async-done(((f32[1,2,2,64,2,512]{5,4,1,2,0,3:T(2,128)}), f32[1,2,2,64,2,512]{5,4,1,2,0,3:T(2,128)S(1)}, u32[]{:S(2)}, u32[]{:S(2)}) %all-to-all-start.5) | async-done | bytes 1048608 | tf_op jit(solution)/shard_map/all_to_all | solution.py:107
  175.2 10.4 %all-to-all-start.1 = ((f32[2,2,2,64,2,512]{5,4,1,0,2,3:T(2,128)}), f32[2,2,2,64,2,512]{5,4,1,0,2,3:T(2,128)S(1)}, u32[]{:S(2)}, u32[]{:S(2)}) async-start(f32[2,2,2,64,2,512]{5,4,1,0,2,3:T(2,128)} %copy.88), calls=%async_computation.1 | async-start | bytes 4194304 | tf_op jit(solution)/shard_map/all_to_all | solution.py:107
  194.1 25.1 %all-to-all-done.1 = f32[2,2,2,64,2,512]{5,4,1,0,2,3:T(2,128)S(1)} async-done(((f32[2,2,2,64,2,512]{5,4,1,0,2,3:T(2,128)}), f32[2,2,2,64,2,512]{5,4,1,0,2,3:T(2,128)S(1)}, u32[]{:S(2)}, u32[]{:S(2)}) %all-to-all-start.1) | async-done | bytes 2097184 | tf_op jit(solution)/shard_map/all_to_all | solution.py:107
  237.2 44.5 %all_to_all.84 = f32[1,2,2,1,128,512]{5,1,2,3,0,4:T(2,128)S(1)} all-to-all(f32[1,2,2,1,128,512]{5,1,2,3,0,4:T(2,128)} %copy.96), channel_id=1, replica_groups=mesh['ctx'=64,'tp'=4] {'ctx'}, dimensions={4} | all-to-all | bytes 2097152 | tf_op jit(solution)/shard_map/all_to_all | solution.py:122
  287.1 32.7 %all_to_all.85 = f32[1,2,2,64,2,512]{5,4,1,2,0,3:T(2,128)S(1)} all-to-all(f32[1,2,2,64,2,512]{5,4,1,2,0,3:T(2,128)S(1)} %copy.100), channel_id=1, replica_groups=mesh['ctx'=64,'tp'=4] {'ctx'}, dimensions={3} | all-to-all | bytes 2097152 | tf_op jit(solution)/shard_map/all_to_all | solution.py:126
  321.8 27.4 %all_gather.3 = bf16[128,2048]{1,0:T(8,128)(2,1)S(1)} all-gather(bf16[128,512]{1,0:T(8,128)(2,1)S(1)} %fusion.50), channel_id=1, replica_groups=mesh['ctx'=64,'tp'=4] {'tp'}, dimensions={1}, use_global_device_ids=true | all-gather | bytes 655360 | tf_op jit(solution)/shard_map/all_gather | solution.py:160
  349.2 4.6 fusion.331
  361.4 2.4 copy.116
  363.8 72.0 %all_to_all.86 = f32[2,2,2,1,128,512]{5,1,0,2,3,4:T(2,128)S(1)} all-to-all(f32[2,2,2,1,128,512]{5,1,0,2,3,4:T(2,128)} %copy.116), channel_id=1, replica_groups=mesh['ctx'=64,'tp'=4] {'ctx'}, dimensions={4} | all-to-all | bytes 4194304 | tf_op jit(solution)/shard_map/all_to_all | solution.py:122
  444.6 3.0 copy.120
  447.6 13.2 %all-to-all-start.7 = ((f32[2,2,2,64,2,512]{5,4,1,0,2,3:T(2,128)}), f32[2,2,2,64,2,512]{5,4,1,0,2,3:T(2,128)S(1)}, u32[]{:S(2)}, u32[]{:S(2)}) async-start(f32[2,2,2,64,2,512]{5,4,1,0,2,3:T(2,128)} %copy.120), calls=%async_computation.8 | async-start | bytes 4194304 | tf_op jit(solution)/shard_map/all_to_all | solution.py:126
  460.8 3.6 convolution_convert_fusion
  464.4 40.7 %all-to-all-done.7 = f32[2,2,2,64,2,512]{5,4,1,0,2,3:T(2,128)S(1)} async-done(((f32[2,2,2,64,2,512]{5,4,1,0,2,3:T(2,128)}), f32[2,2,2,64,2,512]{5,4,1,0,2,3:T(2,128)S(1)}, u32[]{:S(2)}, u32[]{:S(2)}) %all-to-all-start.7) | async-done | bytes 2097184 | tf_op jit(solution)/shard_map/all_to_all | solution.py:126
  507.2 2.7 squeeze.113
  511.5 325.7 %reduce-scatter.5.cloned.1.call-done = f32[32,1024]{1,0:T(8,128)} async-done(((f32[2048,1024]{1,0:T(8,128)}), f32[32,1024]{1,0:T(8,128)}) %reduce-scatter.5.cloned.1.call-update) | async-done | bytes 131088 | tf_op jit(solution)/shard_map/reduce_scatter | solution.py:178
  (117 shorter events, 76.1 us)
Async XLA Ops:
  7.2 1.0 copy-start
  7.2 37.5 %copy-start.8 = (bf16[128,512]{1,0:T(8,128)(2,1)S(1)}, bf16[128,512]{1,0:T(8,128)(2,1)}, u32[]{:S(2)}) copy-start(bf16[128,512]{1,0:T(8,128)(2,1)} %param.6) | copy-start | bytes 393220
  7.2 37.5 %reduce-scatter.3.cloned.1.call-start = ((), (), s32[]{:S(2)}) async-start(), calls=%async_computation.10 | async-start | bytes 1310720 | tf_op jit(solution)/shard_map/reduce_scatter | solution.py:167
  12.9 47.6 %copy-start.10 = (f32[128]{0:T(128)}, f32[128]{0:T(128)S(1)}, u32[]{:S(2)}) copy-start(f32[128]{0:T(128)S(1)} %get-tuple-element.50) | copy-start | bytes 1540
  45.9 14.6 %copy-start.3 = (f32[128,512]{1,0:T(8,128)S(1)}, f32[128,512]{1,0:T(8,128)}, u32[]{:S(2)}) copy-start(f32[128,512]{1,0:T(8,128)} %param.9) | copy-start | bytes 786436
  46.0 14.6 %copy-start.5 = (bf16[128,512]{1,0:T(8,128)(2,1)S(1)}, bf16[128,512]{1,0:T(8,128)(2,1)}, u32[]{:S(2)}) copy-start(bf16[128,512]{1,0:T(8,128)(2,1)} %param.8) | copy-start | bytes 393220
  46.0 14.6 %copy-start.6 = (bf16[128,512]{1,0:T(8,128)(2,1)S(1)}, bf16[128,512]{1,0:T(8,128)(2,1)}, u32[]{:S(2)}) copy-start(bf16[128,512]{1,0:T(8,128)(2,1)} %param.7) | copy-start | bytes 393220
  47.8 44.2 %all-to-all-start.4 = ((f32[1,2,2,1,128,512]{5,2,1,3,0,4:T(2,128)}), f32[1,2,2,1,128,512]{5,2,1,3,0,4:T(2,128)S(1)}, u32[]{:S(2)}, u32[]{:S(2)}) async-start(f32[1,2,2,1,128,512]{5,2,1,3,0,4:T(2,128)} %copy.105), calls=%async_computation.5 | async-start | bytes 2097152 | tf_op jit(solution)/shard_map/all_to_all | solution.py:103
  91.9 39.2 %all-to-all-start = ((f32[2,2,2,1,128,512]{5,2,1,0,3,4:T(2,128)}), f32[2,2,2,1,128,512]{5,2,1,0,3,4:T(2,128)S(1)}, u32[]{:S(2)}, u32[]{:S(2)}) async-start(f32[2,2,2,1,128,512]{5,2,1,0,3,4:T(2,128)} %copy.84), calls=%async_computation | async-start | bytes 4194304 | tf_op jit(solution)/shard_map/all_to_all | solution.py:103
  131.1 43.2 %all-to-all-start.5 = ((f32[1,2,2,64,2,512]{5,4,1,2,0,3:T(2,128)}), f32[1,2,2,64,2,512]{5,4,1,2,0,3:T(2,128)S(1)}, u32[]{:S(2)}, u32[]{:S(2)}) async-start(f32[1,2,2,64,2,512]{5,4,1,2,0,3:T(2,128)} %copy.109), calls=%async_computation.6 | async-start | bytes 2097152 | tf_op jit(solution)/shard_map/all_to_all | solution.py:107
  174.3 1.0 copy-start.1
  175.2 43.9 %all-to-all-start.1 = ((f32[2,2,2,64,2,512]{5,4,1,0,2,3:T(2,128)}), f32[2,2,2,64,2,512]{5,4,1,0,2,3:T(2,128)S(1)}, u32[]{:S(2)}, u32[]{:S(2)}) async-start(f32[2,2,2,64,2,512]{5,4,1,0,2,3:T(2,128)} %copy.88), calls=%async_computation.1 | async-start | bytes 4194304 | tf_op jit(solution)/shard_map/all_to_all | solution.py:107
  185.6 651.5 %reduce-scatter.5.cloned.1.call-start = ((), (), s32[]{:S(2)}) async-start(), calls=%async_computation.11 | async-start | bytes 8519680 | tf_op jit(solution)/shard_map/reduce_scatter | solution.py:178
  232.4 2.5 copy-start.12
  232.4 2.5 copy-start.13
  319.8 1.1 copy-start.4
  319.8 1.1 copy-start.11
  319.8 1.9 copy-start.9
  353.7 1.0 copy-start.2
  358.6 1.3 copy-start.14
  447.6 57.5 %all-to-all-start.7 = ((f32[2,2,2,64,2,512]{5,4,1,0,2,3:T(2,128)}), f32[2,2,2,64,2,512]{5,4,1,0,2,3:T(2,128)S(1)}, u32[]{:S(2)}, u32[]{:S(2)}) async-start(f32[2,2,2,64,2,512]{5,4,1,0,2,3:T(2,128)} %copy.120), calls=%async_computation.8 | async-start | bytes 4194304 | tf_op jit(solution)/shard_map/all_to_all | solution.py:126
  509.9 0.9 copy-start.7
Sparse Core Ops, SparseCore 0:
  12.9 31.6 reduce-scatter.2
  353.9 483.2 reduce-scatter.4
where the time goes:
time: 859 us; the launch traced here: 845 us
  waiting for transfers between devices  488 us (57%)
  blocking collectives  177 us (21%)
  starting transfers between devices  61.9 us (7%)
  matrix products  56 us (7%)
  local copies, waits for them, and re-layouts  38.8 us (5%)
  between operations  15.3 us (2%)
    reduce_scatter x1, waiting for transfers between devices, per_device(): lax.psum_scatter(lax.dot_general(every_channel, grad_out, (((0,), (0,)),...  326 us
    all_to_all x2, blocking collectives, inverse_transform(): lax.all_to_all(values[:, :, :, None], 'ctx', split_axis=4, concat_axis=3,...  117 us
    all_to_all x2, waiting for transfers between devices, forward_transform(): lax.all_to_all(values[:, :, :, None], 'ctx', split_axis=4, concat_axis=3,...  55.6 us
    all_to_all x1, waiting for transfers between devices, inverse_transform(): lax.all_to_all(combined, 'ctx', split_axis=3, concat_axis=4, tiled=True)  40.7 us
    all_to_all x2, waiting for transfers between devices, forward_transform(): lax.all_to_all(combined, 'ctx', split_axis=3, concat_axis=4, tiled=True)  34.3 us
    all_to_all x1, blocking collectives, inverse_transform(): lax.all_to_all(combined, 'ctx', split_axis=3, concat_axis=4, tiled=True)  32.7 us
    reduce_scatter x1, waiting for transfers between devices, per_device(): lax.psum_scatter(partial_value, 'tp', scatter_dimension=1, tiled=True)  31.8 us
    all_to_all x2, starting transfers between devices, forward_transform(): lax.all_to_all(combined, 'ctx', split_axis=3, concat_axis=4, tiled=True)  31 us
  transfers between devices with their start and end apart: 7, of which 7 were waited for; matrix products, arithmetic and copies ran while one was open for 7% of the time, Pallas kernels for 0%

commit v1 on v0

v1 whole, which is shorter than its diff:
```python
import functools

import jax
import jax.numpy as jnp
from jax import lax
from jax.experimental import pallas as pl
from jax.experimental.pallas import tpu as pltpu
from jax.sharding import PartitionSpec as P

f32 = jnp.float32
bf16 = jnp.bfloat16
MESH = pl.DeviceIdType.MESH
OWN = 8
TOK = 128


def dot_nn(a, b):
    return lax.dot_general(a, b, (((1,), (0,)), ((), ())), preferred_element_type=f32)


def dot_nt(a, b):
    return lax.dot_general(a, b, (((1,), (1,)), ((), ())), preferred_element_type=f32)


def kernel(
    dims,
    q_ref,
    k_ref,
    v_ref,
    f_ref,
    w_ref,
    go_ref,
    out_ref,
    gq_ref,
    gk_ref,
    gv_ref,
    gf_ref,
    gw_ref,
    s1_ref,
    r1_ref,
    xf_ref,
    xpad_ref,
    gpad_ref,
    t_ref,
    qt_ref,
    gm_ref,
    ps_ref,
    pr_ref,
    gs_ref,
    gr_ref,
    ys_ref,
    yr_ref,
    pqf_ref,
    pqs_ref,
    pqr_ref,
    mix_ref,
    b_ref,
    a_ref,
    cf_ref,
    cs_ref,
    cr_ref,
    zs_ref,
    zr_ref,
    send_sem,
    recv_sem,
    tp_send,
    tp_recv,
    mx_send,
    mx_recv,
):
    nx, ny, nz, nc, nt = dims
    n = nx * ny * nz * nc
    ch = OWN * n
    cols = go_ref.shape[1]
    gwr = gw_ref.shape[0]
    group = nx * nc
    me = lax.axis_index("ctx")
    tp = lax.axis_index("tp")
    core = me % nc
    zh = me // nc % nz
    yy = me // (nc * nz) % ny
    xx = me // (nc * nz * ny)
    slot = xx * nc + core

    row_id = lax.broadcasted_iota(jnp.int32, (TOK, TOK), 0)
    col_id = lax.broadcasted_iota(jnp.int32, (TOK, TOK), 1)
    eye = (row_id == col_id).astype(f32).astype(bf16)
    rev = (row_id + col_id == TOK - 1).astype(f32).astype(bf16)
    lower = col_id >= row_id

    def remote(src, dst, ssem, rsem, device):
        return pltpu.make_async_remote_copy(
            src_ref=src,
            dst_ref=dst,
            send_sem=ssem,
            recv_sem=rsem,
            device_id=device,
            device_id_type=MESH,
        )

    def wait_rows(ref, rows, sem):
        pltpu.make_async_copy(ref.at[pl.ds(0, rows)], ref.at[pl.ds(0, rows)], sem).wait()

    def spread(src, dst, size, src_block, dst_block, index):
        def one(step, carry):
            peer = (me + step) % n
            remote(
                src.at[pl.ds(pl.multiple_of(src_block(peer) * size, size), size)],
                dst.at[pl.ds(pl.multiple_of(dst_block * size, size), size)],
                send_sem.at[index],
                recv_sem.at[index],
                {"ctx": peer},
            ).start()
            return carry

        lax.fori_loop(1, n, one, 0)

    barrier = pltpu.get_barrier_semaphore()

    def greet(step, carry):
        pl.semaphore_signal(
            barrier, inc=1, device_id={"ctx": (me + step) % n}, device_id_type=MESH
        )
        return carry

    lax.fori_loop(1, n, greet, 0)
    for step in range(1, nt):
        pl.semaphore_signal(
            barrier, inc=1, device_id={"tp": (tp + step) % nt}, device_id_type=MESH
        )

    for j in range(ch // TOK):
        lanes = pl.ds(j * TOK, TOK)
        gated = (k_ref[:, lanes].astype(f32) * v_ref[:, lanes].astype(f32)).astype(bf16)
        gated_t = dot_nt(eye, gated).reshape(TOK // OWN, OWN, TOK)
        filter_t = dot_nt(eye, f_ref[:, lanes].astype(bf16)).reshape(TOK // OWN, OWN, TOK)
        both = jnp.concatenate([gated_t, filter_t], axis=1)
        s1_ref[pl.ds(2 * j * TOK, 2 * TOK), :] = both.reshape(2 * TOK, TOK).astype(bf16)
        qt_ref[pl.ds(j * TOK, TOK), :] = dot_nt(eye, q_ref[:, lanes])

    pl.semaphore_wait(barrier, n - 1 + nt - 1)
    spread(s1_ref, r1_ref, 2 * OWN, lambda peer: peer, me, 0)

    part = min(ch, 256)

    def partial(target, write):
        def rows(i, carry):
            start = pl.multiple_of(target * ch + i * part, part)
            write(
                pl.ds(pl.multiple_of(i * part, part), part),
                dot_nt(w_ref[pl.ds(start, part), :], go_ref[...]),
            )
            return carry

        lax.fori_loop(0, ch // part, rows, 0)

    for step in range(1, nt):
        peer = (tp + step) % nt

        def put(rows, value, step=step):
            ps_ref[step - 1, rows, :] = value.astype(bf16)

        partial(peer, put)
        remote(
            ps_ref.at[step - 1],
            pr_ref.at[step - 1],
            tp_send.at[step - 1],
            tp_recv.at[step - 1],
            {"tp": peer},
        ).start()

    def put_own(rows, value):
        gm_ref[rows, :] = value

    partial(tp, put_own)

    def share(step, carry):
        other = (slot + step) % group
        peer = ((other // nc * ny + yy) * nz + zh) * nc + other % nc
        remote(go_ref, b_ref.at[slot], send_sem.at[4], recv_sem.at[4], {"ctx": peer}).start()
        return carry

    lax.fori_loop(1, group, share, 0)

    for step in range(1, nt):
        remote(
            ps_ref.at[step - 1],
            pr_ref.at[step - 1],
            tp_send.at[step - 1],
            tp_recv.at[step - 1],
            {"tp": (tp + step) % nt},
        ).wait_recv()

    def sum_rows(i, carry):
        rows = pl.ds(pl.multiple_of(i * TOK, TOK), TOK)
        total = gm_ref[rows, :]
        for step in range(1, nt):
            total = total + pr_ref[step - 1, rows, :].astype(f32)
        gm_ref[rows, :] = total
        gs_ref[rows, :] = dot_nn((total * qt_ref[rows, :]).astype(bf16), rev)
        return carry

    lax.fori_loop(0, ch // TOK, sum_rows, 0)
    spread(gs_ref, gr_ref, OWN, lambda peer: peer, n - 1 - me, 1)

    wait_rows(r1_ref, (n - 1) * 2 * OWN, recv_sem.at[0])
    mine = pl.ds(pl.multiple_of(me * 2 * OWN, 2 * OWN), 2 * OWN)
    r1_ref[mine, :] = s1_ref[mine, :]
    xf_ref[...] = r1_ref[...].astype(f32)

    def toeplitz(c, first, lanes):
        def block(d, before):
            line = xf_ref[pl.ds(d * 2 * OWN + first + c, 1), :]
            now = pltpu.roll(
                jnp.broadcast_to(line, (TOK, TOK)), 0, 1, stride=1, stride_axis=0
            )
            t_ref[c, d, :, lanes] = jnp.where(lower, now, before).astype(bf16)
            return now

        lax.fori_loop(0, n, block, jnp.zeros((TOK, TOK), f32))

    def convolve(pad, c, lanes, width):
        def step(e, acc):
            left = jnp.concatenate(
                [pad[c, pl.ds(n - 2 * e, n), :], pad[c, pl.ds(n - 1 - 2 * e, n), :]], axis=1
            ).astype(bf16)
            right = t_ref[c, pl.ds(2 * e, 2), :, lanes].reshape(2 * TOK, width)
            return acc + dot_nn(left, right)

        return lax.fori_loop(0, n // 2, step, jnp.zeros((n, width), f32))

    def forward(c, carry):
        xpad_ref[c, pl.ds(0, n), :] = jnp.zeros((n, TOK), f32)
        xpad_ref[c, pl.ds(n, n), :] = xf_ref[pl.ds(c, n, stride=2 * OWN), :]
        toeplitz(c, OWN, pl.ds(0, TOK))
        ys_ref[pl.ds(c, n, stride=OWN), :] = convolve(xpad_ref, c, pl.ds(0, TOK), TOK)
        return carry

    lax.fori_loop(0, OWN, forward, 0)
    spread(ys_ref, yr_ref, OWN, lambda peer: peer, me, 2)

    def other_blocks(c, carry):
        toeplitz(c, 0, pl.ds(TOK, TOK))
        return carry

    lax.fori_loop(0, OWN, other_blocks, 0)

    wait_rows(yr_ref, (n - 1) * OWN, recv_sem.at[2])
    mine8 = pl.ds(pl.multiple_of(me * OWN, OWN), OWN)
    yr_ref[mine8, :] = ys_ref[mine8, :]
    per = ny * nz * nc * gwr // TOK

    def mix(i, carry):
        rows = pl.ds(pl.multiple_of(i * TOK, TOK), TOK)
        mixed = (qt_ref[rows, :] * yr_ref[rows, :]).astype(bf16)
        mix_ref[pl.ds(pl.multiple_of(tp * ch + i * TOK, TOK), TOK), :] = mixed
        return carry

    lax.fori_loop(0, ch // TOK, mix, 0)
    own_rows = pl.ds(pl.multiple_of(tp * ch, ch), ch)
    for step in range(1, nt):
        remote(
            mix_ref.at[own_rows],
            mix_ref.at[own_rows],
            mx_send.at[step - 1],
            mx_recv.at[step - 1],
            {"tp": (tp + step) % nt},
        ).start()

    wait_rows(gr_ref, (n - 1) * OWN, recv_sem.at[1])
    gr_ref[pl.ds(pl.multiple_of((n - 1 - me) * OWN, OWN), OWN), :] = gs_ref[mine8, :]

    def backward(c, carry):
        gpad_ref[c, pl.ds(0, n), :] = jnp.zeros((n, TOK), f32)
        gpad_ref[c, pl.ds(n, n), :] = gr_ref[pl.ds(c, n, stride=OWN), :]
        acc = convolve(gpad_ref, c, pl.ds(0, 2 * TOK), 2 * TOK)
        pqf_ref[pl.ds(c, n, stride=2 * OWN), :] = acc[:, :TOK]
        pqf_ref[pl.ds(OWN + c, n, stride=2 * OWN), :] = acc[:, TOK:]
        return carry

    lax.fori_loop(0, OWN, backward, 0)
    pqs_ref[...] = pqf_ref[...].astype(bf16)
    spread(pqs_ref, pqr_ref, 2 * OWN, lambda peer: n - 1 - peer, me, 3)

    for step in range(1, nt):
        source = (tp + nt - step) % nt
        rows = pl.ds(pl.multiple_of(source * ch, ch), ch)
        remote(
            mix_ref.at[rows],
            mix_ref.at[rows],
            mx_send.at[step - 1],
            mx_recv.at[step - 1],
            {"tp": (tp + step) % nt},
        ).wait_recv()

    blocks = ny * nz

    def block_rows(other, b):
        index = (other // nc * blocks + b) * nc + other % nc
        return pl.ds(pl.multiple_of(index * gwr, gwr), gwr)

    def feed(step, carry):
        other = (slot + step) % group
        peer = ((other // nc * ny + yy) * nz + zh) * nc + other % nc

        def one(b, inner):
            remote(
                mix_ref.at[block_rows(other, b)],
                a_ref.at[slot, pl.ds(pl.multiple_of(b * gwr, gwr), gwr)],
                send_sem.at[5],
                recv_sem.at[5],
                {"ctx": peer},
            ).start()
            return inner

        lax.fori_loop(0, blocks, one, 0)
        return carry

    lax.fori_loop(1, group, feed, 0)

    wide = min(cols, 256)

    def project(i, carry):
        columns = pl.ds(pl.multiple_of(i * wide, wide), wide)
        acc = jnp.zeros((TOK, wide), f32)
        for source in range(nt):
            rows = pl.ds(source * ch, ch)
            left = dot_nt(eye, mix_ref[rows, :]).astype(bf16)
            acc = acc + dot_nn(left, w_ref[rows, columns])
        out_ref[:, columns] = acc.astype(bf16)
        return carry

    lax.fori_loop(0, cols // wide, project, 0)

    wait_rows(b_ref, group - 1, recv_sem.at[4])
    wait_rows(a_ref, group - 1, recv_sem.at[5])
    b_ref[slot] = go_ref[...]

    def keep(b, carry):
        a_ref[slot, pl.ds(pl.multiple_of(b * gwr, gwr), gwr), :] = mix_ref[
            block_rows(slot, b), :
        ]
        return carry

    lax.fori_loop(0, blocks, keep, 0)
    tall = nz * gwr

    def weight(i, carry):
        columns = pl.ds(pl.multiple_of(i * wide, wide), wide)
        acc = jnp.zeros((blocks * gwr, wide), f32)
        for source in range(group):
            acc = acc + dot_nn(a_ref[source], b_ref[source, :, columns])
        cf_ref[:, columns] = acc
        return carry

    lax.fori_loop(0, cols // wide, weight, 0)
    for y_step in range(1, ny):
        other = (yy + y_step) % ny
        rows = pl.ds(pl.multiple_of(other * tall, tall), tall)
        cs_ref[y_step - 1] = cf_ref[rows, :].astype(bf16)
        peer = ((xx * ny + other) * nz + zh) * nc + core
        remote(
            cs_ref.at[y_step - 1],
            cr_ref.at[y_step - 1],
            send_sem.at[6],
            recv_sem.at[6],
            {"ctx": peer},
        ).start()

    def query(j, carry):
        rows = pl.ds(pl.multiple_of(j * TOK, TOK), TOK)
        grad = (gm_ref[rows, :] * yr_ref[rows, :]).astype(bf16)
        gq_ref[:, rows] = dot_nt(eye, grad).astype(bf16)
        return carry

    lax.fori_loop(0, ch // TOK, query, 0)
    wait_rows(pqr_ref, (n - 1) * 2 * OWN, recv_sem.at[3])
    back = pl.ds(pl.multiple_of((n - 1 - me) * 2 * OWN, 2 * OWN), 2 * OWN)
    pqr_ref[mine, :] = pqs_ref[back, :]

    def finish(j, carry):
        lanes = pl.ds(pl.multiple_of(j * TOK, TOK), TOK)
        both = pqr_ref[pl.ds(pl.multiple_of(2 * j * TOK, TOK), 2 * TOK), :].astype(f32)
        both = both.reshape(TOK // OWN, 2 * OWN, TOK)
        grad_gated = dot_nt(rev, both[:, :OWN].reshape(TOK, TOK).astype(bf16))
        gf_ref[:, lanes] = dot_nt(rev, both[:, OWN:].reshape(TOK, TOK).astype(bf16))
        gk_ref[:, lanes] = (grad_gated * v_ref[:, lanes].astype(f32)).astype(bf16)
        gv_ref[:, lanes] = (grad_gated * k_ref[:, lanes].astype(f32)).astype(bf16)
        return carry

    lax.fori_loop(0, ch // TOK, finish, 0)

    wait_rows(cr_ref, ny - 1, recv_sem.at[6])
    own_z = pl.multiple_of(yy * tall + zh * gwr, gwr)
    far = (zh + 1) % nz
    far_total = cf_ref[pl.ds(pl.multiple_of(yy * tall + far * gwr, gwr), gwr), :]
    own_total = cf_ref[pl.ds(own_z, gwr), :]
    for y_step in range(1, ny):
        far_total = far_total + cr_ref[
            y_step - 1, pl.ds(pl.multiple_of(far * gwr, gwr), gwr), :
        ].astype(f32)
        own_total = own_total + cr_ref[
            y_step - 1, pl.ds(pl.multiple_of(zh * gwr, gwr), gwr), :
        ].astype(f32)
    zs_ref[...] = far_total.astype(bf16)
    gw_ref[...] = own_total
    across = remote(
        zs_ref,
        zr_ref,
        send_sem.at[7],
        recv_sem.at[7],
        {"ctx": ((xx * ny + yy) * nz + far) * nc + core},
    )
    across.start()
    across.wait_recv()
    gw_ref[...] += zr_ref[...].astype(f32)

    wait_rows(s1_ref, (n - 1) * 2 * OWN, send_sem.at[0])
    wait_rows(gs_ref, (n - 1) * OWN, send_sem.at[1])
    wait_rows(ys_ref, (n - 1) * OWN, send_sem.at[2])
    wait_rows(pqs_ref, (n - 1) * 2 * OWN, send_sem.at[3])
    wait_rows(b_ref, group - 1, send_sem.at[4])
    wait_rows(a_ref, group - 1, send_sem.at[5])
    wait_rows(cs_ref, ny - 1, send_sem.at[6])
    across.wait_send()
    for step in range(1, nt):
        peer = {"tp": (tp + step) % nt}
        remote(
            ps_ref.at[step - 1],
            pr_ref.at[step - 1],
            tp_send.at[step - 1],
            tp_recv.at[step - 1],
            peer,
        ).wait_send()
        remote(
            mix_ref.at[own_rows],
            mix_ref.at[own_rows],
            mx_send.at[step - 1],
            mx_recv.at[step - 1],
            peer,
        ).wait_send()


def per_device(dims, q, k, v, f, w, go):
    nx, ny, nz, nc, nt = dims
    n = nx * ny * nz * nc
    ch = OWN * n
    every = ch * nt
    cols = go.shape[1]
    gwr = every // n
    group = nx * nc
    tall = nz * gwr
    vmem = pl.BlockSpec(memory_space=pltpu.VMEM)
    return pl.pallas_call(
        functools.partial(kernel, dims),
        out_shape=(
            jax.ShapeDtypeStruct((TOK, cols), bf16),
            jax.ShapeDtypeStruct((TOK, ch), bf16),
            jax.ShapeDtypeStruct((TOK, ch), bf16),
            jax.ShapeDtypeStruct((TOK, ch), bf16),
            jax.ShapeDtypeStruct((TOK, ch), f32),
            jax.ShapeDtypeStruct((gwr, cols), f32),
        ),
        in_specs=[vmem] * 6,
        out_specs=[vmem] * 6,
        scratch_shapes=[
            pltpu.VMEM((2 * ch, TOK), bf16),
            pltpu.VMEM((2 * ch, TOK), bf16),
            pltpu.VMEM((2 * ch, TOK), f32),
            pltpu.VMEM((OWN, 2 * n, TOK), f32),
            pltpu.VMEM((OWN, 2 * n, TOK), f32),
            pltpu.VMEM((OWN, n, TOK, 2 * TOK), bf16),
            pltpu.VMEM((ch, TOK), f32),
            pltpu.VMEM((ch, TOK), f32),
            pltpu.VMEM((nt - 1, ch, TOK), bf16),
            pltpu.VMEM((nt - 1, ch, TOK), bf16),
            pltpu.VMEM((ch, TOK), f32),
            pltpu.VMEM((ch, TOK), f32),
            pltpu.VMEM((ch, TOK), f32),
            pltpu.VMEM((ch, TOK), f32),
            pltpu.VMEM((2 * ch, TOK), f32),
            pltpu.VMEM((2 * ch, TOK), bf16),
            pltpu.VMEM((2 * ch, TOK), bf16),
            pltpu.VMEM((every, TOK), bf16),
            pltpu.VMEM((group, TOK, cols), bf16),
            pltpu.VMEM((group, ny * nz * gwr, TOK), bf16),
            pltpu.VMEM((ny * nz * gwr, cols), f32),
            pltpu.VMEM((ny - 1, tall, cols), bf16),
            pltpu.VMEM((ny - 1, tall, cols), bf16),
            pltpu.VMEM((gwr, cols), bf16),
            pltpu.VMEM((gwr, cols), bf16),
            pltpu.SemaphoreType.DMA((8,)),
            pltpu.SemaphoreType.DMA((8,)),
            pltpu.SemaphoreType.DMA((nt - 1,)),
            pltpu.SemaphoreType.DMA((nt - 1,)),
            pltpu.SemaphoreType.DMA((nt - 1,)),
            pltpu.SemaphoreType.DMA((nt - 1,)),
        ],
        compiler_params=pltpu.CompilerParams(
            collective_id=0, has_side_effects=True, vmem_limit_bytes=56 * 1024 * 1024
        ),
    )(q, k, v, f, w, go)


def solution(mesh, dims=(4, 4, 2, 2, 4)):
    return jax.shard_map(
        functools.partial(per_device, dims),
        mesh=mesh,
        in_specs=(
            P("ctx", "tp"),
            P("ctx", "tp"),
            P("ctx", "tp"),
            P("ctx", "tp"),
            P(None, "tp"),
            P("ctx", "tp"),
        ),
        out_specs=(P("ctx", "tp"),) * 6,
        check_vma=False,
    )
```

time: 859 us -> 238 us (0.28); the launches traced: 845 us -> 235 us
  waiting for transfers between devices: 488 us -> 0 us
  Pallas kernels: 0 us -> 224 us
  blocking collectives: 177 us -> 0 us
  starting transfers between devices: 61.9 us -> 0 us
  matrix products: 56 us -> 0 us
  local copies, waits for them, and re-layouts: 38.8 us -> 9.61 us
  between operations: 15.3 us -> 0.64 us
    reduce_scatter x2 -> x0, waiting for transfers between devices: 357 us -> none  [the longest x1 326 us: per_device(): lax.psum_scatter(lax.dot_general(every_channel, grad_out, (((0,), (0,)),...]
    pallas_call x0 -> x1, Pallas kernels: none -> 224 us  [per_device(): pl.pallas_call(functools.partial(kernel, dims), out_shape=(jax.ShapeDtype...]
    all_to_all x3 -> x0, blocking collectives: 149 us -> none  [the longest x2 117 us: inverse_transform(): lax.all_to_all(values[:, :, :, None], 'ctx', split_axis=4, concat_axis=3,...]
    all_to_all x5 -> x0, waiting for transfers between devices: 131 us -> none  [the longest x2 55.6 us: forward_transform(): lax.all_to_all(values[:, :, :, None], 'ctx', split_axis=4, concat_axis=3,...]
    all_to_all x5 -> x0, starting transfers between devices: 61.6 us -> none  [the longest x2 31 us: forward_transform(): lax.all_to_all(combined, 'ctx', split_axis=3, concat_axis=4, tiled=True)]
    dot_general x35 -> x0, matrix products: 56 us -> none  [the longest x16 21.7 us: apply_table(): return jnp.einsum('km,srmc->srkc', matrix, part, precision=highest)]
    all_gather x1 -> x0, blocking collectives: 27.4 us -> none  [per_device(): every_channel = lax.all_gather(mixed_rows, 'tp', axis=1, tiled=True)]
    another operation x8 -> x0, local copies, waits for them, and re-layouts: 10.5 us -> none  [the longest x4 8.53 us: cross_mix(): return jnp.stack([new_real, new_imag], axis=2)]
  transfers between devices with their start and end apart: 7 -> 0, of which waited for: 7 -> 0; matrix products, arithmetic and copies ran while one was open for 7% -> 0% of each run, Pallas kernels for 0% -> 0%
where the time goes in v1:
time: 238 us; the launch traced here: 235 us
  Pallas kernels  224 us (94%)
  local copies, waits for them, and re-layouts  9.61 us (4%)
    pallas_call x1, Pallas kernels, per_device(): pl.pallas_call(functools.partial(kernel, dims), out_shape=(jax.ShapeDtype...  224 us
    unnamed x6, local copies, waits for them, and re-layouts  9.61 us

profile of v1, /device:TPU:96, one launch (start us, length us, event | category | flops | bytes accessed | tf_op | source)
XLA Modules:
  0.0 234.7 jit_solution(7463852050637262436)
XLA Ops:
  0.6 224.5 %shard_map.109 = (bf16[128,1024]{1,0:T(8,128)(2,1)}, bf16[128,512]{1,0:T(8,128)(2,1)}, bf16[128,512]{1,0:T(8,128)(2,1)}, bf16[128,512]{1,0:T(8,128)(2,1)}, f32[128,512]{1,0:T(8,128)}, /*index=5*/f32[32,1024]{1,0:T(8,128)}) custom-call(bf16[128,512]{1,0:T(8,128)(2,1)} %q_ref.1, bf16[128,512]{1,0:T(8,128)(2,1)} %k_ref.1, bf16[128,512]{1,0:T(8,128)(2,1)} %v_ref.1, ...), custom_call_target="tpu_custom_call" | custom-call | tf_op jit(solution)/shard_map/pallas_call | solution.py:454
  225.1 1.7 copy.18
  226.8 1.6 copy.19
  228.4 1.6 copy.20
  229.9 1.6 copy.21
  231.5 1.7 copy.22
  233.2 1.6 copy.23

commit v2 on v1

--- a/solution.py
+++ b/solution.py
@@ -217,17 +217,13 @@
             t_ref[c, d, :, lanes] = jnp.where(lower, now, before).astype(bf16)
             return now
 
-        lax.fori_loop(0, n, block, jnp.zeros((TOK, TOK), f32))
+        lax.fori_loop(0, n, block, jnp.zeros((TOK, TOK), f32), unroll=min(n, 32))
 
     def convolve(pad, c, lanes, width):
-        def step(e, acc):
-            left = jnp.concatenate(
-                [pad[c, pl.ds(n - 2 * e, n), :], pad[c, pl.ds(n - 1 - 2 * e, n), :]], axis=1
-            ).astype(bf16)
-            right = t_ref[c, pl.ds(2 * e, 2), :, lanes].reshape(2 * TOK, width)
-            return acc + dot_nn(left, right)
-
-        return lax.fori_loop(0, n // 2, step, jnp.zeros((n, width), f32))
+        left = jnp.concatenate(
+            [pad[c, pl.ds(n - i, n), :].astype(bf16) for i in range(n)], axis=1
+        )
+        return dot_nn(left, t_ref[c, :, :, lanes].reshape(n * TOK, width))
 
     def forward(c, carry):
         xpad_ref[c, pl.ds(0, n), :] = jnp.zeros((n, TOK), f32)

time: 238 us -> 108 us (0.45); the launches traced: 235 us -> 108 us
  Pallas kernels: 224 us -> 98 us
    pallas_call x1, Pallas kernels: 224 us -> 98 us  [per_device(): pl.pallas_call(functools.partial(kernel, dims), out_shape=(jax.ShapeDtype...]
where the time goes in v2:
time: 108 us
  Pallas kernels  98 us (91%)
  local copies, waits for them, and re-layouts  9.61 us (9%)
    pallas_call x1, Pallas kernels, per_device(): pl.pallas_call(functools.partial(kernel, dims), out_shape=(jax.ShapeDtype...  98 us
    unnamed x6, local copies, waits for them, and re-layouts  9.61 us

profile of v2, /device:TPU:96, one launch (start us, length us, event | category | flops | bytes accessed | tf_op | source)
XLA Modules:
  0.0 108.3 jit_solution(8637025616507186405)
XLA Ops:
  0.6 98.0 %shard_map.109 = (bf16[128,1024]{1,0:T(8,128)(2,1)}, bf16[128,512]{1,0:T(8,128)(2,1)}, bf16[128,512]{1,0:T(8,128)(2,1)}, bf16[128,512]{1,0:T(8,128)(2,1)}, f32[128,512]{1,0:T(8,128)}, /*index=5*/f32[32,1024]{1,0:T(8,128)}) custom-call(bf16[128,512]{1,0:T(8,128)(2,1)} %q_ref.1, bf16[128,512]{1,0:T(8,128)(2,1)} %k_ref.1, bf16[128,512]{1,0:T(8,128)(2,1)} %v_ref.1, ...), custom_call_target="tpu_custom_call" | custom-call | tf_op jit(solution)/shard_map/pallas_call | solution.py:450
  98.7 1.7 %copy.18 = bf16[128,1024]{1,0:T(8,128)(2,1)} copy(bf16[128,1024]{1,0:T(8,128)(2,1)} %get-tuple-element.12) | data formatting | bytes 524288
  100.3 1.6 %copy.19 = bf16[128,512]{1,0:T(8,128)(2,1)} copy(bf16[128,512]{1,0:T(8,128)(2,1)} %get-tuple-element.13) | data formatting | bytes 262144
  101.9 1.6 %copy.20 = bf16[128,512]{1,0:T(8,128)(2,1)} copy(bf16[128,512]{1,0:T(8,128)(2,1)} %get-tuple-element.14) | data formatting | bytes 262144
  103.5 1.6 %copy.21 = bf16[128,512]{1,0:T(8,128)(2,1)} copy(bf16[128,512]{1,0:T(8,128)(2,1)} %get-tuple-element.15) | data formatting | bytes 262144
  105.0 1.7 %copy.22 = f32[128,512]{1,0:T(8,128)} copy(f32[128,512]{1,0:T(8,128)} %get-tuple-element.16) | data formatting | bytes 524288
  106.7 1.6 %copy.23 = f32[32,1024]{1,0:T(8,128)} copy(f32[32,1024]{1,0:T(8,128)} %get-tuple-element.17) | data formatting | bytes 262144

commit v3 on v2

--- a/solution.py
+++ b/solution.py
@@ -28,7 +28,7 @@
     k_ref,
     v_ref,
     f_ref,
-    w_ref,
+    wh_ref,
     go_ref,
     out_ref,
     gq_ref,
@@ -54,6 +54,8 @@
     pqs_ref,
     pqr_ref,
     mix_ref,
+    ml_ref,
+    w_ref,
     b_ref,
     a_ref,
     cf_ref,
@@ -67,6 +69,13 @@
     tp_recv,
     mx_send,
     mx_recv,
+    a_send,
+    a_recv,
+    c_send,
+    c_recv,
+    z_send,
+    z_recv,
+    local_sem,
 ):
     nx, ny, nz, nc, nt = dims
     n = nx * ny * nz * nc
@@ -115,6 +124,10 @@
 
         lax.fori_loop(1, n, one, 0)
 
+    def member(step):
+        other = (slot + step) % group
+        return ((other // nc * ny + yy) * nz + zh) * nc + other % nc
+
     barrier = pltpu.get_barrier_semaphore()
 
     def greet(step, carry):
@@ -128,6 +141,9 @@
         pl.semaphore_signal(
             barrier, inc=1, device_id={"tp": (tp + step) % nt}, device_id_type=MESH
         )
+
+    weight_copy = pltpu.make_async_copy(wh_ref, w_ref, local_sem)
+    weight_copy.start()
 
     for j in range(ch // TOK):
         lanes = pl.ds(j * TOK, TOK)
@@ -141,7 +157,8 @@
     pl.semaphore_wait(barrier, n - 1 + nt - 1)
     spread(s1_ref, r1_ref, 2 * OWN, lambda peer: peer, me, 0)
 
-    part = min(ch, 256)
+    part = min(ch, 512)
+    weight_copy.wait()
 
     def partial(target, write):
         def rows(i, carry):
@@ -175,36 +192,16 @@
     partial(tp, put_own)
 
     def share(step, carry):
-        other = (slot + step) % group
-        peer = ((other // nc * ny + yy) * nz + zh) * nc + other % nc
-        remote(go_ref, b_ref.at[slot], send_sem.at[4], recv_sem.at[4], {"ctx": peer}).start()
+        remote(
+            go_ref, b_ref.at[slot], send_sem.at[4], recv_sem.at[4], {"ctx": member(step)}
+        ).start()
         return carry
 
     lax.fori_loop(1, group, share, 0)
-
-    for step in range(1, nt):
-        remote(
-            ps_ref.at[step - 1],
-            pr_ref.at[step - 1],
-            tp_send.at[step - 1],
-            tp_recv.at[step - 1],
-            {"tp": (tp + step) % nt},
-        ).wait_recv()
-
-    def sum_rows(i, carry):
-        rows = pl.ds(pl.multiple_of(i * TOK, TOK), TOK)
-        total = gm_ref[rows, :]
-        for step in range(1, nt):
-            total = total + pr_ref[step - 1, rows, :].astype(f32)
-        gm_ref[rows, :] = total
-        gs_ref[rows, :] = dot_nn((total * qt_ref[rows, :]).astype(bf16), rev)
-        return carry
-
-    lax.fori_loop(0, ch // TOK, sum_rows, 0)
-    spread(gs_ref, gr_ref, OWN, lambda peer: peer, n - 1 - me, 1)
 
     wait_rows(r1_ref, (n - 1) * 2 * OWN, recv_sem.at[0])
     mine = pl.ds(pl.multiple_of(me * 2 * OWN, 2 * OWN), 2 * OWN)
+    mine8 = pl.ds(pl.multiple_of(me * OWN, OWN), OWN)
     r1_ref[mine, :] = s1_ref[mine, :]
     xf_ref[...] = r1_ref[...].astype(f32)
 
@@ -217,7 +214,7 @@
             t_ref[c, d, :, lanes] = jnp.where(lower, now, before).astype(bf16)
             return now
 
-        lax.fori_loop(0, n, block, jnp.zeros((TOK, TOK), f32), unroll=min(n, 32))
+        lax.fori_loop(0, n, block, jnp.zeros((TOK, TOK), f32), unroll=n)
 
     def convolve(pad, c, lanes, width):
         left = jnp.concatenate(
@@ -235,33 +232,87 @@
     lax.fori_loop(0, OWN, forward, 0)
     spread(ys_ref, yr_ref, OWN, lambda peer: peer, me, 2)
 
-    def other_blocks(c, carry):
-        toeplitz(c, 0, pl.ds(TOK, TOK))
-        return carry
-
-    lax.fori_loop(0, OWN, other_blocks, 0)
+    for step in range(1, nt):
+        remote(
+            ps_ref.at[step - 1],
+            pr_ref.at[step - 1],
+            tp_send.at[step - 1],
+            tp_recv.at[step - 1],
+            {"tp": (tp + step) % nt},
+        ).wait_recv()
+
+    def sum_rows(i, carry):
+        rows = pl.ds(pl.multiple_of(i * TOK, TOK), TOK)
+        total = gm_ref[rows, :]
+        for step in range(1, nt):
+            total = total + pr_ref[step - 1, rows, :].astype(f32)
+        gm_ref[rows, :] = total
+        gs_ref[rows, :] = dot_nn((total * qt_ref[rows, :]).astype(bf16), rev)
+        return carry
+
+    lax.fori_loop(0, ch // TOK, sum_rows, 0)
+    spread(gs_ref, gr_ref, OWN, lambda peer: peer, n - 1 - me, 1)
 
     wait_rows(yr_ref, (n - 1) * OWN, recv_sem.at[2])
-    mine8 = pl.ds(pl.multiple_of(me * OWN, OWN), OWN)
     yr_ref[mine8, :] = ys_ref[mine8, :]
-    per = ny * nz * nc * gwr // TOK
+    blocks = ny * nz
+    per = TOK // (nc * gwr)
 
     def mix(i, carry):
         rows = pl.ds(pl.multiple_of(i * TOK, TOK), TOK)
         mixed = (qt_ref[rows, :] * yr_ref[rows, :]).astype(bf16)
-        mix_ref[pl.ds(pl.multiple_of(tp * ch + i * TOK, TOK), TOK), :] = mixed
+        mix_ref[tp, pl.ds(i * per, per)] = mixed.reshape(per, nc, gwr, TOK)
         return carry
 
     lax.fori_loop(0, ch // TOK, mix, 0)
-    own_rows = pl.ds(pl.multiple_of(tp * ch, ch), ch)
+
     for step in range(1, nt):
         remote(
-            mix_ref.at[own_rows],
-            mix_ref.at[own_rows],
+            mix_ref.at[tp],
+            mix_ref.at[tp],
             mx_send.at[step - 1],
             mx_recv.at[step - 1],
             {"tp": (tp + step) % nt},
         ).start()
+
+    def feed(source):
+        for core_step in range(nc):
+            to_core = (core + core_step) % nc
+            copy = remote(
+                mix_ref.at[source, :, to_core],
+                a_ref.at[slot],
+                a_send,
+                a_recv,
+                {"ctx": ((source * ny + yy) * nz + zh) * nc + to_core},
+            )
+            if core_step == 0:
+
+                @pl.when(xx != source)
+                def _(copy=copy):
+                    copy.start()
+
+            else:
+                copy.start()
+
+    def other_blocks(c, carry):
+        toeplitz(c, 0, pl.ds(TOK, TOK))
+        return carry
+
+    feed(tp)
+    done = 0
+    for step in range(1, nt):
+        until = OWN * step // (nt - 1)
+        lax.fori_loop(done, until, other_blocks, 0)
+        done = until
+        source = (tp + nt - step) % nt
+        remote(
+            mix_ref.at[source],
+            mix_ref.at[source],
+            mx_send.at[step - 1],
+            mx_recv.at[step - 1],
+            {"tp": (tp + step) % nt},
+        ).wait_recv()
+        feed(source)
 
     wait_rows(gr_ref, (n - 1) * OWN, recv_sem.at[1])
     gr_ref[pl.ds(pl.multiple_of((n - 1 - me) * OWN, OWN), OWN), :] = gs_ref[mine8, :]
@@ -276,92 +327,85 @@
 
     lax.fori_loop(0, OWN, backward, 0)
     pqs_ref[...] = pqf_ref[...].astype(bf16)
-    spread(pqs_ref, pqr_ref, 2 * OWN, lambda peer: n - 1 - peer, me, 3)
-
-    for step in range(1, nt):
-        source = (tp + nt - step) % nt
-        rows = pl.ds(pl.multiple_of(source * ch, ch), ch)
-        remote(
-            mix_ref.at[rows],
-            mix_ref.at[rows],
-            mx_send.at[step - 1],
-            mx_recv.at[step - 1],
-            {"tp": (tp + step) % nt},
-        ).wait_recv()
-
-    blocks = ny * nz
-
-    def block_rows(other, b):
-        index = (other // nc * blocks + b) * nc + other % nc
-        return pl.ds(pl.multiple_of(index * gwr, gwr), gwr)
-
-    def feed(step, carry):
-        other = (slot + step) % group
-        peer = ((other // nc * ny + yy) * nz + zh) * nc + other % nc
-
-        def one(b, inner):
-            remote(
-                mix_ref.at[block_rows(other, b)],
-                a_ref.at[slot, pl.ds(pl.multiple_of(b * gwr, gwr), gwr)],
-                send_sem.at[5],
-                recv_sem.at[5],
-                {"ctx": peer},
-            ).start()
-            return inner
-
-        lax.fori_loop(0, blocks, one, 0)
-        return carry
-
-    lax.fori_loop(1, group, feed, 0)
+
+    wait_rows(b_ref, group - 1, recv_sem.at[4])
+    wait_rows(a_ref, group - 1, a_recv)
+    b_ref[slot] = go_ref[...]
+    a_ref[slot] = mix_ref[xx, :, core]
 
     wide = min(cols, 256)
-
-    def project(i, carry):
-        columns = pl.ds(pl.multiple_of(i * wide, wide), wide)
-        acc = jnp.zeros((TOK, wide), f32)
-        for source in range(nt):
-            rows = pl.ds(source * ch, ch)
-            left = dot_nt(eye, mix_ref[rows, :]).astype(bf16)
-            acc = acc + dot_nn(left, w_ref[rows, columns])
-        out_ref[:, columns] = acc.astype(bf16)
-        return carry
-
-    lax.fori_loop(0, cols // wide, project, 0)
-
-    wait_rows(b_ref, group - 1, recv_sem.at[4])
-    wait_rows(a_ref, group - 1, recv_sem.at[5])
-    b_ref[slot] = go_ref[...]
-
-    def keep(b, carry):
-        a_ref[slot, pl.ds(pl.multiple_of(b * gwr, gwr), gwr), :] = mix_ref[
-            block_rows(slot, b), :
-        ]
-        return carry
-
-    lax.fori_loop(0, blocks, keep, 0)
+    tiles = cols // wide
     tall = nz * gwr
+
+    def send_tile(i, y_step):
+        other = (yy + y_step) % ny
+        return remote(
+            cs_ref.at[i, y_step - 1],
+            cr_ref.at[i, y_step - 1],
+            c_send.at[i],
+            c_recv.at[i],
+            {"ctx": ((xx * ny + other) * nz + zh) * nc + core},
+        )
 
     def weight(i, carry):
         columns = pl.ds(pl.multiple_of(i * wide, wide), wide)
         acc = jnp.zeros((blocks * gwr, wide), f32)
         for source in range(group):
-            acc = acc + dot_nn(a_ref[source], b_ref[source, :, columns])
-        cf_ref[:, columns] = acc
-        return carry
-
-    lax.fori_loop(0, cols // wide, weight, 0)
-    for y_step in range(1, ny):
-        other = (yy + y_step) % ny
-        rows = pl.ds(pl.multiple_of(other * tall, tall), tall)
-        cs_ref[y_step - 1] = cf_ref[rows, :].astype(bf16)
-        peer = ((xx * ny + other) * nz + zh) * nc + core
-        remote(
-            cs_ref.at[y_step - 1],
-            cr_ref.at[y_step - 1],
-            send_sem.at[6],
-            recv_sem.at[6],
-            {"ctx": peer},
-        ).start()
+            left = a_ref[source].reshape(blocks * gwr, TOK)
+            acc = acc + dot_nn(left, b_ref[source, :, columns])
+        cf_ref[i] = acc
+        for y_step in range(1, ny):
+            other = (yy + y_step) % ny
+            rows = pl.ds(pl.multiple_of(other * tall, tall), tall)
+            cs_ref[i, y_step - 1] = cf_ref[i, rows, :].astype(bf16)
+            send_tile(i, y_step).start()
+        return carry
+
+    lax.fori_loop(0, tiles, weight, 0)
+
+    spread(pqs_ref, pqr_ref, 2 * OWN, lambda peer: n - 1 - peer, me, 3)
+
+    far = (zh + 1) % nz
+
+    def across(i):
+        return remote(
+            zs_ref.at[i],
+            zr_ref.at[i],
+            z_send.at[i],
+            z_recv.at[i],
+            {"ctx": ((xx * ny + yy) * nz + far) * nc + core},
+        )
+
+    def over_y(i, carry):
+        pltpu.make_async_copy(cr_ref.at[i], cr_ref.at[i], c_recv.at[i]).wait()
+
+        def total(level):
+            rows = pl.ds(pl.multiple_of(level * gwr, gwr), gwr)
+            value = cf_ref[i, pl.ds(pl.multiple_of(yy * tall + level * gwr, gwr), gwr), :]
+            for y_step in range(1, ny):
+                value = value + cr_ref[i, y_step - 1, rows, :].astype(f32)
+            return value
+
+        zs_ref[i] = total(far).astype(bf16)
+        across(i).start()
+        gw_ref[:, pl.ds(pl.multiple_of(i * wide, wide), wide)] = total(zh)
+        return carry
+
+    lax.fori_loop(0, tiles, over_y, 0)
+
+    def turn(source, carry):
+        left = dot_nt(eye, mix_ref[source].reshape(ch, TOK)).astype(bf16)
+        ml_ref[:, pl.ds(pl.multiple_of(source * ch, ch), ch)] = left
+        return carry
+
+    lax.fori_loop(0, nt, turn, 0)
+
+    def project(i, carry):
+        columns = pl.ds(pl.multiple_of(i * wide, wide), wide)
+        out_ref[:, columns] = dot_nn(ml_ref[...], w_ref[:, columns]).astype(bf16)
+        return carry
+
+    lax.fori_loop(0, tiles, project, 0)
 
     def query(j, carry):
         rows = pl.ds(pl.multiple_of(j * TOK, TOK), TOK)
@@ -386,39 +430,28 @@
 
     lax.fori_loop(0, ch // TOK, finish, 0)
 
-    wait_rows(cr_ref, ny - 1, recv_sem.at[6])
-    own_z = pl.multiple_of(yy * tall + zh * gwr, gwr)
-    far = (zh + 1) % nz
-    far_total = cf_ref[pl.ds(pl.multiple_of(yy * tall + far * gwr, gwr), gwr), :]
-    own_total = cf_ref[pl.ds(own_z, gwr), :]
-    for y_step in range(1, ny):
-        far_total = far_total + cr_ref[
-            y_step - 1, pl.ds(pl.multiple_of(far * gwr, gwr), gwr), :
-        ].astype(f32)
-        own_total = own_total + cr_ref[
-            y_step - 1, pl.ds(pl.multiple_of(zh * gwr, gwr), gwr), :
-        ].astype(f32)
-    zs_ref[...] = far_total.astype(bf16)
-    gw_ref[...] = own_total
-    across = remote(
-        zs_ref,
-        zr_ref,
-        send_sem.at[7],
-        recv_sem.at[7],
-        {"ctx": ((xx * ny + yy) * nz + far) * nc + core},
-    )
-    across.start()
-    across.wait_recv()
-    gw_ref[...] += zr_ref[...].astype(f32)
+    def over_z(i, carry):
+        across(i).wait_recv()
+        columns = pl.ds(pl.multiple_of(i * wide, wide), wide)
+        gw_ref[:, columns] = gw_ref[:, columns] + zr_ref[i].astype(f32)
+        return carry
+
+    lax.fori_loop(0, tiles, over_z, 0)
 
     wait_rows(s1_ref, (n - 1) * 2 * OWN, send_sem.at[0])
     wait_rows(gs_ref, (n - 1) * OWN, send_sem.at[1])
     wait_rows(ys_ref, (n - 1) * OWN, send_sem.at[2])
     wait_rows(pqs_ref, (n - 1) * 2 * OWN, send_sem.at[3])
     wait_rows(b_ref, group - 1, send_sem.at[4])
-    wait_rows(a_ref, group - 1, send_sem.at[5])
-    wait_rows(cs_ref, ny - 1, send_sem.at[6])
-    across.wait_send()
+
+    wait_rows(a_ref, group - 1, a_send)
+
+    def left_tile(i, carry):
+        pltpu.make_async_copy(cs_ref.at[i], cs_ref.at[i], c_send.at[i]).wait()
+        across(i).wait_send()
+        return carry
+
+    lax.fori_loop(0, tiles, left_tile, 0)
     for step in range(1, nt):
         peer = {"tp": (tp + step) % nt}
         remote(
@@ -429,12 +462,34 @@
             peer,
         ).wait_send()
         remote(
-            mix_ref.at[own_rows],
-            mix_ref.at[own_rows],
+            mix_ref.at[tp],
+            mix_ref.at[tp],
             mx_send.at[step - 1],
             mx_recv.at[step - 1],
             peer,
         ).wait_send()
+
+
+def place_kernel(*refs):
+    copies = [
+        pltpu.make_async_copy(refs[i], refs[6 + i], refs[12].at[i]) for i in range(6)
+    ]
+    for copy in copies:
+        copy.start()
+    for copy in copies:
+        copy.wait()
+
+
+def place(arrays):
+    anywhere = pl.BlockSpec(memory_space=pl.ANY)
+    return pl.pallas_call(
+        place_kernel,
+        out_shape=tuple(jax.ShapeDtypeStruct(a.shape, a.dtype) for a in arrays),
+        in_specs=[anywhere] * 6,
+        out_specs=[pl.BlockSpec(memory_space=pltpu.VMEM)] * 6,
+        scratch_shapes=[pltpu.SemaphoreType.DMA((6,))],
+        compiler_params=pltpu.CompilerParams(vmem_limit_bytes=60 * 1024 * 1024),
+    )(*arrays)
 
 
 def per_device(dims, q, k, v, f, w, go):
@@ -446,8 +501,10 @@
     gwr = every // n
     group = nx * nc
     tall = nz * gwr
+    wide = min(cols, 256)
+    tiles = cols // wide
     vmem = pl.BlockSpec(memory_space=pltpu.VMEM)
-    return pl.pallas_call(
+    results = pl.pallas_call(
         functools.partial(kernel, dims),
         out_shape=(
             jax.ShapeDtypeStruct((TOK, cols), bf16),
@@ -457,7 +514,7 @@
             jax.ShapeDtypeStruct((TOK, ch), f32),
             jax.ShapeDtypeStruct((gwr, cols), f32),
         ),
-        in_specs=[vmem] * 6,
+        in_specs=[vmem] * 4 + [pl.BlockSpec(memory_space=pl.ANY), vmem],
         out_specs=[vmem] * 6,
         scratch_shapes=[
             pltpu.VMEM((2 * ch, TOK), bf16),
@@ -477,25 +534,35 @@
             pltpu.VMEM((2 * ch, TOK), f32),
             pltpu.VMEM((2 * ch, TOK), bf16),
             pltpu.VMEM((2 * ch, TOK), bf16),
-            pltpu.VMEM((every, TOK), bf16),
+            pltpu.VMEM((nt, ny * nz, nc, gwr, TOK), bf16),
+            pltpu.VMEM((TOK, every), bf16),
+            pltpu.VMEM((every, cols), bf16),
             pltpu.VMEM((group, TOK, cols), bf16),
-            pltpu.VMEM((group, ny * nz * gwr, TOK), bf16),
-            pltpu.VMEM((ny * nz * gwr, cols), f32),
-            pltpu.VMEM((ny - 1, tall, cols), bf16),
-            pltpu.VMEM((ny - 1, tall, cols), bf16),
-            pltpu.VMEM((gwr, cols), bf16),
-            pltpu.VMEM((gwr, cols), bf16),
-            pltpu.SemaphoreType.DMA((8,)),
-            pltpu.SemaphoreType.DMA((8,)),
+            pltpu.VMEM((group, ny * nz, gwr, TOK), bf16),
+            pltpu.VMEM((tiles, ny * nz * gwr, wide), f32),
+            pltpu.VMEM((tiles, ny - 1, tall, wide), bf16),
+            pltpu.VMEM((tiles, ny - 1, tall, wide), bf16),
+            pltpu.VMEM((tiles, gwr, wide), bf16),
+            pltpu.VMEM((tiles, gwr, wide), bf16),
+            pltpu.SemaphoreType.DMA((5,)),
+            pltpu.SemaphoreType.DMA((5,)),
             pltpu.SemaphoreType.DMA((nt - 1,)),
             pltpu.SemaphoreType.DMA((nt - 1,)),
             pltpu.SemaphoreType.DMA((nt - 1,)),
             pltpu.SemaphoreType.DMA((nt - 1,)),
+            pltpu.SemaphoreType.DMA,
+            pltpu.SemaphoreType.DMA,
+            pltpu.SemaphoreType.DMA((tiles,)),
+            pltpu.SemaphoreType.DMA((tiles,)),
+            pltpu.SemaphoreType.DMA((tiles,)),
+            pltpu.SemaphoreType.DMA((tiles,)),
+            pltpu.SemaphoreType.DMA,
         ],
         compiler_params=pltpu.CompilerParams(
             collective_id=0, has_side_effects=True, vmem_limit_bytes=56 * 1024 * 1024
         ),
     )(q, k, v, f, w, go)
+    return place(results)
 
 
 def solution(mesh, dims=(4, 4, 2, 2, 4)):

time: 108 us -> 88.8 us (0.82)
  Pallas kernels: 98 us -> 88.1 us
  local copies, waits for them, and re-layouts: 9.61 us -> 0 us
    pallas_call x1, Pallas kernels: 98 us -> 85.8 us  [per_device(): pl.pallas_call(functools.partial(kernel, dims), out_shape=(jax.ShapeDtype...]
    unnamed x6 -> x0, local copies, waits for them, and re-layouts: 9.61 us -> none
    pallas_call x0 -> x1, Pallas kernels: none -> 2.24 us  [place(): pl.pallas_call(place_kernel, out_shape=tuple((jax.ShapeDtypeStruct(a.shap...]
where the time goes in v3:
time: 88.8 us; the launch traced here: 88.7 us
  Pallas kernels  88.1 us (99%)
    pallas_call x1, Pallas kernels, per_device(): pl.pallas_call(functools.partial(kernel, dims), out_shape=(jax.ShapeDtype...  85.8 us
    pallas_call x1, Pallas kernels, place(): pl.pallas_call(place_kernel, out_shape=tuple((jax.ShapeDtypeStruct(a.shap...  2.24 us

profile of v3, /device:TPU:96, one launch (start us, length us, event | category | flops | bytes accessed | tf_op | source)
XLA Modules:
  0.0 88.7 jit_solution(17216935745447308600)
XLA Ops:
  0.6 85.8 %shard_map.109 = (bf16[128,1024]{1,0:T(8,128)(2,1)}, bf16[128,512]{1,0:T(8,128)(2,1)}, bf16[128,512]{1,0:T(8,128)(2,1)}, bf16[128,512]{1,0:T(8,128)(2,1)}, f32[128,512]{1,0:T(8,128)}, /*index=5*/f32[32,1024]{1,0:T(8,128)}) custom-call(bf16[128,512]{1,0:T(8,128)(2,1)} %q_ref.1, bf16[128,512]{1,0:T(8,128)(2,1)} %k_ref.1, bf16[128,512]{1,0:T(8,128)(2,1)} %v_ref.1, ...), custom_call_target="tpu_custom_call" | custom-call | tf_op jit(solution)/shard_map/pallas_call | solution.py:507
  86.5 2.2 %shard_map.110 = (bf16[128,1024]{1,0:T(8,128)(2,1)}, bf16[128,512]{1,0:T(8,128)(2,1)}, bf16[128,512]{1,0:T(8,128)(2,1)}, bf16[128,512]{1,0:T(8,128)(2,1)}, f32[128,512]{1,0:T(8,128)}, /*index=5*/f32[32,1024]{1,0:T(8,128)}) custom-call(bf16[128,1024]{1,0:T(8,128)(2,1)} %get-tuple-element.12.refs_0_, bf16[128,512]{1,0:T(8,128)(2,1)} %get-tuple-element.13.refs_1_, ...), custom_call_target="tpu_custom_call" | custom-call | tf_op jit(solution)/shard_map/pallas_call | solution.py:485

commit v4 on v3

--- a/solution.py
+++ b/solution.py
@@ -46,9 +46,12 @@
     gm_ref,
     ps_ref,
     pr_ref,
-    gs_ref,
+    gsb_ref,
+    grb_ref,
     gr_ref,
     ys_ref,
+    ysb_ref,
+    yrb_ref,
     yr_ref,
     pqf_ref,
     pqs_ref,
@@ -69,6 +72,8 @@
     tp_recv,
     mx_send,
     mx_recv,
+    b_send,
+    b_recv,
     a_send,
     a_recv,
     c_send,
@@ -110,6 +115,20 @@
     def wait_rows(ref, rows, sem):
         pltpu.make_async_copy(ref.at[pl.ds(0, rows)], ref.at[pl.ds(0, rows)], sem).wait()
 
+    def spread8(src, dst, dst_block, index):
+        def one(step, carry):
+            peer = (me + step) % n
+            remote(
+                src.at[peer],
+                dst.at[dst_block],
+                send_sem.at[index],
+                recv_sem.at[index],
+                {"ctx": peer},
+            ).start()
+            return carry
+
+        lax.fori_loop(1, n, one, 0)
+
     def spread(src, dst, size, src_block, dst_block, index):
         def one(step, carry):
             peer = (me + step) % n
@@ -172,36 +191,39 @@
         lax.fori_loop(0, ch // part, rows, 0)
 
     for step in range(1, nt):
-        peer = (tp + step) % nt
 
         def put(rows, value, step=step):
             ps_ref[step - 1, rows, :] = value.astype(bf16)
 
-        partial(peer, put)
+        partial((tp + step) % nt, put)
+
+    def put_own(rows, value):
+        gm_ref[rows, :] = value
+
+    partial(tp, put_own)
+
+    wait_rows(r1_ref, (n - 1) * 2 * OWN, recv_sem.at[0])
+    mine = pl.ds(pl.multiple_of(me * 2 * OWN, 2 * OWN), 2 * OWN)
+    for step in range(1, nt):
         remote(
             ps_ref.at[step - 1],
             pr_ref.at[step - 1],
             tp_send.at[step - 1],
             tp_recv.at[step - 1],
-            {"tp": peer},
+            {"tp": (tp + step) % nt},
         ).start()
 
-    def put_own(rows, value):
-        gm_ref[rows, :] = value
-
-    partial(tp, put_own)
-
-    def share(step, carry):
-        remote(
-            go_ref, b_ref.at[slot], send_sem.at[4], recv_sem.at[4], {"ctx": member(step)}
-        ).start()
-        return carry
-
-    lax.fori_loop(1, group, share, 0)
-
-    wait_rows(r1_ref, (n - 1) * 2 * OWN, recv_sem.at[0])
-    mine = pl.ds(pl.multiple_of(me * 2 * OWN, 2 * OWN), 2 * OWN)
-    mine8 = pl.ds(pl.multiple_of(me * OWN, OWN), OWN)
+    def along(step):
+        return remote(
+            go_ref,
+            b_ref.at[slot],
+            b_send,
+            b_recv,
+            {"ctx": (((xx + step) % nx * ny + yy) * nz + zh) * nc + core},
+        )
+
+    for step in range(1, nx):
+        along(step).start()
     r1_ref[mine, :] = s1_ref[mine, :]
     xf_ref[...] = r1_ref[...].astype(f32)
 
@@ -230,7 +252,8 @@
         return carry
 
     lax.fori_loop(0, OWN, forward, 0)
-    spread(ys_ref, yr_ref, OWN, lambda peer: peer, me, 2)
+    ysb_ref[...] = ys_ref[...].reshape(n, OWN, TOK).astype(bf16)
+    spread8(ysb_ref, yrb_ref, me, 2)
 
     for step in range(1, nt):
         remote(
@@ -247,14 +270,35 @@
         for step in range(1, nt):
             total = total + pr_ref[step - 1, rows, :].astype(f32)
         gm_ref[rows, :] = total
-        gs_ref[rows, :] = dot_nn((total * qt_ref[rows, :]).astype(bf16), rev)
+        back = dot_nn((total * qt_ref[rows, :]).astype(bf16), rev)
+        gsb_ref[pl.ds(i * (TOK // OWN), TOK // OWN)] = back.reshape(
+            TOK // OWN, OWN, TOK
+        ).astype(bf16)
         return carry
 
     lax.fori_loop(0, ch // TOK, sum_rows, 0)
-    spread(gs_ref, gr_ref, OWN, lambda peer: peer, n - 1 - me, 1)
-
-    wait_rows(yr_ref, (n - 1) * OWN, recv_sem.at[2])
-    yr_ref[mine8, :] = ys_ref[mine8, :]
+    spread8(gsb_ref, grb_ref, n - 1 - me, 1)
+
+    wait_rows(b_ref, nx - 1, b_recv)
+    b_ref[slot] = go_ref[...]
+
+    def to_core(step, x_step):
+        block = b_ref.at[(xx + x_step) % nx * nc + core]
+        return remote(
+            block,
+            block,
+            send_sem.at[4],
+            recv_sem.at[4],
+            {"ctx": me - core + (core + step) % nc},
+        )
+
+    for step in range(1, nc):
+        for x_step in range(nx):
+            to_core(step, x_step).start()
+
+    wait_rows(yrb_ref, n - 1, recv_sem.at[2])
+    yrb_ref[me] = ysb_ref[me]
+    yr_ref[...] = yrb_ref[...].astype(f32).reshape(ch, TOK)
     blocks = ny * nz
     per = TOK // (nc * gwr)
 
@@ -266,21 +310,38 @@
 
     lax.fori_loop(0, ch // TOK, mix, 0)
 
-    for step in range(1, nt):
-        remote(
-            mix_ref.at[tp],
-            mix_ref.at[tp],
-            mx_send.at[step - 1],
-            mx_recv.at[step - 1],
-            {"tp": (tp + step) % nt},
-        ).start()
-
-    def feed(source):
+    half = blocks // 2
+
+    def pass_on(source, way, hop, piece):
+        rows = mix_ref.at[source, pl.ds(piece * half, half)]
+        return remote(
+            rows,
+            rows,
+            mx_send.at[way, hop, piece],
+            mx_recv.at[way, hop, piece],
+            {"tp": jnp.clip(tp + (1 - 2 * way), 0, nt - 1)},
+        )
+
+    def has_next(way):
+        return tp < nt - 1 if way == 0 else tp > 0
+
+    def has_hop(way, hop):
+        return tp >= hop if way == 0 else tp + hop < nt
+
+    for piece in range(2):
+        for way in range(2):
+
+            @pl.when(has_next(way))
+            def _(way=way, piece=piece):
+                pass_on(tp, way, 0, piece).start()
+
+    def feed(source, piece):
+        part_rows = pl.ds(piece * half, half)
         for core_step in range(nc):
             to_core = (core + core_step) % nc
             copy = remote(
-                mix_ref.at[source, :, to_core],
-                a_ref.at[slot],
+                mix_ref.at[source, part_rows, to_core],
+                a_ref.at[slot, part_rows],
                 a_send,
                 a_recv,
                 {"ctx": ((source * ny + yy) * nz + zh) * nc + to_core},
@@ -298,24 +359,31 @@
         toeplitz(c, 0, pl.ds(TOK, TOK))
         return carry
 
-    feed(tp)
+    feed(tp, 0)
+    feed(tp, 1)
     done = 0
-    for step in range(1, nt):
-        until = OWN * step // (nt - 1)
+    for hop in range(1, nt):
+        until = OWN * hop // (nt - 1)
         lax.fori_loop(done, until, other_blocks, 0)
         done = until
-        source = (tp + nt - step) % nt
-        remote(
-            mix_ref.at[source],
-            mix_ref.at[source],
-            mx_send.at[step - 1],
-            mx_recv.at[step - 1],
-            {"tp": (tp + step) % nt},
-        ).wait_recv()
-        feed(source)
-
-    wait_rows(gr_ref, (n - 1) * OWN, recv_sem.at[1])
-    gr_ref[pl.ds(pl.multiple_of((n - 1 - me) * OWN, OWN), OWN), :] = gs_ref[mine8, :]
+        for piece in range(2):
+            for way in range(2):
+
+                @pl.when(has_hop(way, hop))
+                def _(way=way, hop=hop, piece=piece):
+                    source = tp - hop * (1 - 2 * way)
+                    pass_on(source, way, hop - 1, piece).wait_recv()
+                    if hop < nt - 1:
+
+                        @pl.when(has_next(way))
+                        def _():
+                            pass_on(source, way, hop, piece).start()
+
+                    feed(source, piece)
+
+    wait_rows(grb_ref, n - 1, recv_sem.at[1])
+    grb_ref[n - 1 - me] = gsb_ref[me]
+    gr_ref[...] = grb_ref[...].astype(f32).reshape(ch, TOK)
 
     def backward(c, carry):
         gpad_ref[c, pl.ds(0, n), :] = jnp.zeros((n, TOK), f32)
@@ -328,9 +396,9 @@
     lax.fori_loop(0, OWN, backward, 0)
     pqs_ref[...] = pqf_ref[...].astype(bf16)
 
-    wait_rows(b_ref, group - 1, recv_sem.at[4])
+    if nc > 1:
+        wait_rows(b_ref, nx * (nc - 1), recv_sem.at[4])
     wait_rows(a_ref, group - 1, a_recv)
-    b_ref[slot] = go_ref[...]
     a_ref[slot] = mix_ref[xx, :, core]
 
     wide = min(cols, 256)
@@ -439,10 +507,12 @@
     lax.fori_loop(0, tiles, over_z, 0)
 
     wait_rows(s1_ref, (n - 1) * 2 * OWN, send_sem.at[0])
-    wait_rows(gs_ref, (n - 1) * OWN, send_sem.at[1])
-    wait_rows(ys_ref, (n - 1) * OWN, send_sem.at[2])
+    wait_rows(gsb_ref, n - 1, send_sem.at[1])
+    wait_rows(ysb_ref, n - 1, send_sem.at[2])
     wait_rows(pqs_ref, (n - 1) * 2 * OWN, send_sem.at[3])
-    wait_rows(b_ref, group - 1, send_sem.at[4])
+    wait_rows(b_ref, nx - 1, b_send)
+    if nc > 1:
+        wait_rows(b_ref, nx * (nc - 1), send_sem.at[4])
 
     wait_rows(a_ref, group - 1, a_send)
 
@@ -461,13 +531,13 @@
             tp_recv.at[step - 1],
             peer,
         ).wait_send()
-        remote(
-            mix_ref.at[tp],
-            mix_ref.at[tp],
-            mx_send.at[step - 1],
-            mx_recv.at[step - 1],
-            peer,
-        ).wait_send()
+    for hop in range(nt - 1):
+        for piece in range(2):
+            for way in range(2):
+
+                @pl.when(has_next(way) & has_hop(way, hop))
+                def _(way=way, hop=hop, piece=piece):
+                    pass_on(tp - hop * (1 - 2 * way), way, hop, piece).wait_send()
 
 
 def place_kernel(*refs):
@@ -527,9 +597,12 @@
             pltpu.VMEM((ch, TOK), f32),
             pltpu.VMEM((nt - 1, ch, TOK), bf16),
             pltpu.VMEM((nt - 1, ch, TOK), bf16),
+            pltpu.VMEM((n, OWN, TOK), bf16),
+            pltpu.VMEM((n, OWN, TOK), bf16),
             pltpu.VMEM((ch, TOK), f32),
             pltpu.VMEM((ch, TOK), f32),
-            pltpu.VMEM((ch, TOK), f32),
+            pltpu.VMEM((n, OWN, TOK), bf16),
+            pltpu.VMEM((n, OWN, TOK), bf16),
             pltpu.VMEM((ch, TOK), f32),
             pltpu.VMEM((2 * ch, TOK), f32),
             pltpu.VMEM((2 * ch, TOK), bf16),
@@ -548,8 +621,10 @@
             pltpu.SemaphoreType.DMA((5,)),
             pltpu.SemaphoreType.DMA((nt - 1,)),
             pltpu.SemaphoreType.DMA((nt - 1,)),
-            pltpu.SemaphoreType.DMA((nt - 1,)),
-            pltpu.SemaphoreType.DMA((nt - 1,)),
+            pltpu.SemaphoreType.DMA((2, nt - 1, 2)),
+            pltpu.SemaphoreType.DMA((2, nt - 1, 2)),
+            pltpu.SemaphoreType.DMA,
+            pltpu.SemaphoreType.DMA,
             pltpu.SemaphoreType.DMA,
             pltpu.SemaphoreType.DMA,
             pltpu.SemaphoreType.DMA((tiles,)),

time: 88.8 us -> 83 us (0.935)
  the two profiles are of different devices: /device:TPU:96 before, /device:TPU:6 now
where the time goes in v4:
time: 83 us; the launch traced here: 82.9 us
  Pallas kernels  82.2 us (99%)
    pallas_call x1, Pallas kernels, per_device(): pl.pallas_call(functools.partial(kernel, dims), out_shape=(jax.ShapeDtype...  80 us
    pallas_call x1, Pallas kernels, place(): pl.pallas_call(place_kernel, out_shape=tuple((jax.ShapeDtypeStruct(a.shap...  2.24 us

profile of v4, /device:TPU:6, one launch (start us, length us, event | category | flops | bytes accessed | tf_op | source)
XLA Modules:
  0.0 82.9 jit_solution(9252702651791260307)
XLA Ops:
  0.6 80.0 %shard_map.109 = (bf16[128,1024]{1,0:T(8,128)(2,1)}, bf16[128,512]{1,0:T(8,128)(2,1)}, bf16[128,512]{1,0:T(8,128)(2,1)}, bf16[128,512]{1,0:T(8,128)(2,1)}, f32[128,512]{1,0:T(8,128)}, /*index=5*/f32[32,1024]{1,0:T(8,128)}) custom-call(bf16[128,512]{1,0:T(8,128)(2,1)} %q_ref.1, bf16[128,512]{1,0:T(8,128)(2,1)} %k_ref.1, bf16[128,512]{1,0:T(8,128)(2,1)} %v_ref.1, ...), custom_call_target="tpu_custom_call" | custom-call | tf_op jit(solution)/shard_map/pallas_call | solution.py:577
  80.6 2.2 %shard_map.110 = (bf16[128,1024]{1,0:T(8,128)(2,1)}, bf16[128,512]{1,0:T(8,128)(2,1)}, bf16[128,512]{1,0:T(8,128)(2,1)}, bf16[128,512]{1,0:T(8,128)(2,1)}, f32[128,512]{1,0:T(8,128)}, /*index=5*/f32[32,1024]{1,0:T(8,128)}) custom-call(bf16[128,1024]{1,0:T(8,128)(2,1)} %get-tuple-element.12.refs_0_, bf16[128,512]{1,0:T(8,128)(2,1)} %get-tuple-element.13.refs_1_, ...), custom_call_target="tpu_custom_call" | custom-call | tf_op jit(solution)/shard_map/pallas_call | solution.py:555

commit v5 on v4

--- a/solution.py
+++ b/solution.py
@@ -24,11 +24,22 @@
 
 def kernel(
     dims,
+    qh_ref,
+    kh_ref,
+    vh_ref,
+    fh_ref,
+    wh_ref,
+    goh_ref,
+    outh_ref,
+    gqh_ref,
+    gkh_ref,
+    gvh_ref,
+    gfh_ref,
+    gwh_ref,
     q_ref,
     k_ref,
     v_ref,
     f_ref,
-    wh_ref,
     go_ref,
     out_ref,
     gq_ref,
@@ -115,9 +126,21 @@
     def wait_rows(ref, rows, sem):
         pltpu.make_async_copy(ref.at[pl.ds(0, rows)], ref.at[pl.ds(0, rows)], sem).wait()
 
+    def each_peer(body):
+        plane = n // nz
+        place = me // (nz * nc) * nc + core
+
+        def one(step, carry):
+            level = (zh + nz - 1 - step // plane) % nz
+            other = (place + step % plane) % plane
+            body((other // nc * nz + level) * nc + other % nc)
+            return carry
+
+        lax.fori_loop(0, n - plane, one, 0)
+        lax.fori_loop(n - plane + 1, n, one, 0)
+
     def spread8(src, dst, dst_block, index):
-        def one(step, carry):
-            peer = (me + step) % n
+        def send(peer):
             remote(
                 src.at[peer],
                 dst.at[dst_block],
@@ -125,13 +148,11 @@
                 recv_sem.at[index],
                 {"ctx": peer},
             ).start()
-            return carry
-
-        lax.fori_loop(1, n, one, 0)
+
+        each_peer(send)
 
     def spread(src, dst, size, src_block, dst_block, index):
-        def one(step, carry):
-            peer = (me + step) % n
+        def send(peer):
             remote(
                 src.at[pl.ds(pl.multiple_of(src_block(peer) * size, size), size)],
                 dst.at[pl.ds(pl.multiple_of(dst_block * size, size), size)],
@@ -139,13 +160,8 @@
                 recv_sem.at[index],
                 {"ctx": peer},
             ).start()
-            return carry
-
-        lax.fori_loop(1, n, one, 0)
-
-    def member(step):
-        other = (slot + step) % group
-        return ((other // nc * ny + yy) * nz + zh) * nc + other % nc
+
+        each_peer(send)
 
     barrier = pltpu.get_barrier_semaphore()
 
@@ -161,8 +177,21 @@
             barrier, inc=1, device_id={"tp": (tp + step) % nt}, device_id_type=MESH
         )
 
-    weight_copy = pltpu.make_async_copy(wh_ref, w_ref, local_sem)
-    weight_copy.start()
+    def bring(index, src, dst):
+        copy = pltpu.make_async_copy(src, dst, local_sem.at[index])
+        copy.start()
+        return copy
+
+    key_copy = bring(0, kh_ref, k_ref)
+    value_copy = bring(1, vh_ref, v_ref)
+    filter_copy = bring(2, fh_ref, f_ref)
+    query_copy = bring(3, qh_ref, q_ref)
+    grad_copy = bring(4, goh_ref, go_ref)
+    weight_copy = bring(5, wh_ref, w_ref)
+    key_copy.wait()
+    value_copy.wait()
+    filter_copy.wait()
+    query_copy.wait()
 
     for j in range(ch // TOK):
         lanes = pl.ds(j * TOK, TOK)
@@ -177,6 +206,7 @@
     spread(s1_ref, r1_ref, 2 * OWN, lambda peer: peer, me, 0)
 
     part = min(ch, 512)
+    grad_copy.wait()
     weight_copy.wait()
 
     def partial(target, write):
@@ -278,23 +308,6 @@
 
     lax.fori_loop(0, ch // TOK, sum_rows, 0)
     spread8(gsb_ref, grb_ref, n - 1 - me, 1)
-
-    wait_rows(b_ref, nx - 1, b_recv)
-    b_ref[slot] = go_ref[...]
-
-    def to_core(step, x_step):
-        block = b_ref.at[(xx + x_step) % nx * nc + core]
-        return remote(
-            block,
-            block,
-            send_sem.at[4],
-            recv_sem.at[4],
-            {"ctx": me - core + (core + step) % nc},
-        )
-
-    for step in range(1, nc):
-        for x_step in range(nx):
-            to_core(step, x_step).start()
 
     wait_rows(yrb_ref, n - 1, recv_sem.at[2])
     yrb_ref[me] = ysb_ref[me]
@@ -361,6 +374,24 @@
 
     feed(tp, 0)
     feed(tp, 1)
+
+    wait_rows(b_ref, nx - 1, b_recv)
+    b_ref[slot] = go_ref[...]
+
+    def to_core(step, x_step):
+        block = b_ref.at[(xx + x_step) % nx * nc + core]
+        return remote(
+            block,
+            block,
+            send_sem.at[4],
+            recv_sem.at[4],
+            {"ctx": me - core + (core + step) % nc},
+        )
+
+    for step in range(1, nc):
+        for x_step in range(nx):
+            to_core(step, x_step).start()
+
     done = 0
     for hop in range(1, nt):
         until = OWN * hop // (nt - 1)
@@ -482,6 +513,7 @@
         return carry
 
     lax.fori_loop(0, ch // TOK, query, 0)
+    leaving = [bring(6, out_ref, outh_ref), bring(7, gq_ref, gqh_ref)]
     wait_rows(pqr_ref, (n - 1) * 2 * OWN, recv_sem.at[3])
     back = pl.ds(pl.multiple_of((n - 1 - me) * 2 * OWN, 2 * OWN), 2 * OWN)
     pqr_ref[mine, :] = pqs_ref[back, :]
@@ -498,6 +530,12 @@
 
     lax.fori_loop(0, ch // TOK, finish, 0)
 
+    leaving += [
+        bring(8, gk_ref, gkh_ref),
+        bring(9, gv_ref, gvh_ref),
+        bring(10, gf_ref, gfh_ref),
+    ]
+
     def over_z(i, carry):
         across(i).wait_recv()
         columns = pl.ds(pl.multiple_of(i * wide, wide), wide)
@@ -506,6 +544,10 @@
 
     lax.fori_loop(0, tiles, over_z, 0)
 
+    leaving.append(bring(11, gw_ref, gwh_ref))
+
+    for copy in leaving:
+        copy.wait()
     wait_rows(s1_ref, (n - 1) * 2 * OWN, send_sem.at[0])
     wait_rows(gsb_ref, n - 1, send_sem.at[1])
     wait_rows(ysb_ref, n - 1, send_sem.at[2])
@@ -573,7 +615,7 @@
     tall = nz * gwr
     wide = min(cols, 256)
     tiles = cols // wide
-    vmem = pl.BlockSpec(memory_space=pltpu.VMEM)
+    anywhere = pl.BlockSpec(memory_space=pl.ANY)
     results = pl.pallas_call(
         functools.partial(kernel, dims),
         out_shape=(
@@ -584,9 +626,20 @@
             jax.ShapeDtypeStruct((TOK, ch), f32),
             jax.ShapeDtypeStruct((gwr, cols), f32),
         ),
-        in_specs=[vmem] * 4 + [pl.BlockSpec(memory_space=pl.ANY), vmem],
-        out_specs=[vmem] * 6,
+        in_specs=[anywhere] * 6,
+        out_specs=[anywhere] * 6,
         scratch_shapes=[
+            pltpu.VMEM((TOK, ch), bf16),
+            pltpu.VMEM((TOK, ch), bf16),
+            pltpu.VMEM((TOK, ch), bf16),
+            pltpu.VMEM((TOK, ch), f32),
+            pltpu.VMEM((TOK, cols), bf16),
+            pltpu.VMEM((TOK, cols), bf16),
+            pltpu.VMEM((TOK, ch), bf16),
+            pltpu.VMEM((TOK, ch), bf16),
+            pltpu.VMEM((TOK, ch), bf16),
+            pltpu.VMEM((TOK, ch), f32),
+            pltpu.VMEM((gwr, cols), f32),
             pltpu.VMEM((2 * ch, TOK), bf16),
             pltpu.VMEM((2 * ch, TOK), bf16),
             pltpu.VMEM((2 * ch, TOK), f32),
@@ -631,7 +684,7 @@
             pltpu.SemaphoreType.DMA((tiles,)),
             pltpu.SemaphoreType.DMA((tiles,)),
             pltpu.SemaphoreType.DMA((tiles,)),
-            pltpu.SemaphoreType.DMA,
+            pltpu.SemaphoreType.DMA((12,)),
         ],
         compiler_params=pltpu.CompilerParams(
             collective_id=0, has_side_effects=True, vmem_limit_bytes=56 * 1024 * 1024

time: 83 us -> 80.5 us (0.970)
  the two profiles are of different devices: /device:TPU:6 before, /device:TPU:96 now
where the time goes in v5:
time: 80.5 us; the launch traced here: 79.7 us
  Pallas kernels  79 us (98%)
    pallas_call x1, Pallas kernels, per_device(): pl.pallas_call(functools.partial(kernel, dims), out_shape=(jax.ShapeDtype...  76.8 us
    pallas_call x1, Pallas kernels, place(): pl.pallas_call(place_kernel, out_shape=tuple((jax.ShapeDtypeStruct(a.shap...  2.24 us

profile of v5, /device:TPU:96, one launch (start us, length us, event | category | flops | bytes accessed | tf_op | source)
XLA Modules:
  0.0 79.7 jit_solution(18243047964716561030)
XLA Ops:
  0.6 76.8 %shard_map.109 = (bf16[128,1024]{1,0:T(8,128)(2,1)}, bf16[128,512]{1,0:T(8,128)(2,1)}, bf16[128,512]{1,0:T(8,128)(2,1)}, bf16[128,512]{1,0:T(8,128)(2,1)}, f32[128,512]{1,0:T(8,128)}, /*index=5*/f32[32,1024]{1,0:T(8,128)}) custom-call(bf16[128,512]{1,0:T(8,128)(2,1)} %qh_ref.1, bf16[128,512]{1,0:T(8,128)(2,1)} %kh_ref.1, bf16[128,512]{1,0:T(8,128)(2,1)} %vh_ref.1, ...), custom_call_target="tpu_custom_call" | custom-call | tf_op jit(solution)/shard_map/pallas_call | solution.py:619
  77.4 2.2 %shard_map.110 = (bf16[128,1024]{1,0:T(8,128)(2,1)}, bf16[128,512]{1,0:T(8,128)(2,1)}, bf16[128,512]{1,0:T(8,128)(2,1)}, bf16[128,512]{1,0:T(8,128)(2,1)}, f32[128,512]{1,0:T(8,128)}, /*index=5*/f32[32,1024]{1,0:T(8,128)}) custom-call(bf16[128,1024]{1,0:T(8,128)(2,1)} %get-tuple-element.12.refs_0_, bf16[128,512]{1,0:T(8,128)(2,1)} %get-tuple-element.13.refs_1_, ...), custom_call_target="tpu_custom_call" | custom-call | tf_op jit(solution)/shard_map/pallas_call | solution.py:597

commit v6 on v5

--- a/solution.py
+++ b/solution.py
@@ -252,8 +252,6 @@
             {"ctx": (((xx + step) % nx * ny + yy) * nz + zh) * nc + core},
         )
 
-    for step in range(1, nx):
-        along(step).start()
     r1_ref[mine, :] = s1_ref[mine, :]
     xf_ref[...] = r1_ref[...].astype(f32)
 
@@ -284,6 +282,8 @@
     lax.fori_loop(0, OWN, forward, 0)
     ysb_ref[...] = ys_ref[...].reshape(n, OWN, TOK).astype(bf16)
     spread8(ysb_ref, yrb_ref, me, 2)
+    for step in range(1, nx):
+        along(step).start()
 
     for step in range(1, nt):
         remote(

time: 80.5 us -> 83.9 us (1.042)
  the two profiles are of different devices: /device:TPU:96 before, /device:TPU:6 now
where the time goes in v6:
time: 83.9 us; the launch traced here: 83.8 us
  Pallas kernels  83.2 us (99%)
    pallas_call x1, Pallas kernels, per_device(): pl.pallas_call(functools.partial(kernel, dims), out_shape=(jax.ShapeDtype...  80.9 us
    pallas_call x1, Pallas kernels, place(): pl.pallas_call(place_kernel, out_shape=tuple((jax.ShapeDtypeStruct(a.shap...  2.24 us

profile of v6, /device:TPU:6, one launch (start us, length us, event | category | flops | bytes accessed | tf_op | source)
XLA Modules:
  0.0 83.8 jit_solution(1647336468503314450)
XLA Ops:
  0.6 80.9 %shard_map.109 = (bf16[128,1024]{1,0:T(8,128)(2,1)}, bf16[128,512]{1,0:T(8,128)(2,1)}, bf16[128,512]{1,0:T(8,128)(2,1)}, bf16[128,512]{1,0:T(8,128)(2,1)}, f32[128,512]{1,0:T(8,128)}, /*index=5*/f32[32,1024]{1,0:T(8,128)}) custom-call(bf16[128,512]{1,0:T(8,128)(2,1)} %qh_ref.1, bf16[128,512]{1,0:T(8,128)(2,1)} %kh_ref.1, bf16[128,512]{1,0:T(8,128)(2,1)} %vh_ref.1, ...), custom_call_target="tpu_custom_call" | custom-call | tf_op jit(solution)/shard_map/pallas_call | solution.py:619
  81.6 2.2 %shard_map.110 = (bf16[128,1024]{1,0:T(8,128)(2,1)}, bf16[128,512]{1,0:T(8,128)(2,1)}, bf16[128,512]{1,0:T(8,128)(2,1)}, bf16[128,512]{1,0:T(8,128)(2,1)}, f32[128,512]{1,0:T(8,128)}, /*index=5*/f32[32,1024]{1,0:T(8,128)}) custom-call(bf16[128,1024]{1,0:T(8,128)(2,1)} %get-tuple-element.12.refs_0_, bf16[128,512]{1,0:T(8,128)(2,1)} %get-tuple-element.13.refs_1_, ...), custom_call_target="tpu_custom_call" | custom-call | tf_op jit(solution)/shard_map/pallas_call | solution.py:597
